TPU v7x, 256 devices: a whole 4x4x8 slice. The times are simulated.
256 devices in a mesh: slab: 64 (over x, z, core), cam: 4 (over y).
Axes of the slice: x: 4, y: 4, z: 8, core: 2. Of those that a mesh axis runs over, the one named last changes fastest.
Arguments:
- jac_cam: float32 [18, 16384, 128], P(None, ('slab', 'cam')), may hold values from -0.24 to 0.24
- jac_point: float32 [6, 16384, 128], P(None, ('slab', 'cam')), may hold values from -2.7 to 2.7
- point_ids: int32 [16384, 128], P(('slab', 'cam')), may hold values from 0 to 16383
- block_cam: int32 [16384], P(('slab', 'cam')), may hold values from 0 to 3071, as said below
- block_fill: int32 [16384], P(('slab', 'cam')), may hold values from 16 to 128
- rhs: float32 [9, 12288], P(None, ('slab', 'cam'))
Outputs:
- solution: float32 [9, 12288], P(None, ('slab', 'cam'))
- residual: float32 [9, 12288], P(None, ('slab', 'cam'))
Inputs may be any that keep to these rules, and one draw needn't show every extreme that they name: `block_cam`: within one device's 64 blocks the camera numbers never fall; each device's first block has camera 0 and its last camera 3072 - 1.
All inputs are finite; a program needn't handle non-finite values.
Results may differ from a plain program's by a relative error of at most 0.0003.
Values sent between devices are 32-bit elements; how exact they have to be, the bound alone decides.
A program may use at most 128 MiB of HBM per device.

v0:
```python
import jax
import jax.numpy as jnp
from jax import lax
from jax.sharding import PartitionSpec as P

PTS = 16384
ITERS = 2


MU = 1.0
LAMBDA = 0.5


def cofactors(vv):
    v00 = vv[0] + MU
    v01 = vv[1]
    v02 = vv[2]
    v11 = vv[3] + MU
    v12 = vv[4]
    v22 = vv[5] + MU
    c00 = v11 * v22 - v12 * v12
    c01 = v02 * v12 - v01 * v22
    c02 = v01 * v12 - v02 * v11
    c11 = v00 * v22 - v02 * v02
    c12 = v01 * v02 - v00 * v12
    c22 = v00 * v11 - v01 * v01
    det = v00 * c00 + v01 * c01 + v02 * c02
    return jnp.stack([c00, c01, c02, c11, c12, c22, det])


def solve_points(cof, q):
    det = cof[6]
    w0 = (cof[0] * q[0] + cof[1] * q[1] + cof[2] * q[2]) / det
    w1 = (cof[1] * q[0] + cof[3] * q[1] + cof[4] * q[2]) / det
    w2 = (cof[2] * q[0] + cof[4] * q[1] + cof[5] * q[2]) / det
    return jnp.stack([w0, w1, w2])


def precond_dot(residual, precond_res):
    return lax.psum(jnp.sum(residual * precond_res), ("slab", "cam"))


def local(jac_cam, jac_point, point_ids, block_cam, block_fill, rhs):
    highest = lax.Precision.HIGHEST
    blocks, slots = point_ids.shape
    live = (lax.broadcasted_iota(jnp.int32, (blocks, slots), 1) < block_fill[:, None]).astype(
        jnp.float32
    )
    jcam = (jac_cam * live[None]).reshape(2, 9, blocks, slots)
    jpt = (jac_point * live[None]).reshape(2, 3, blocks, slots)
    flat_ids = point_ids.reshape(-1)
    cluster = rhs.shape[1] * lax.axis_size("slab")
    one_hot = (block_cam[:, None] == lax.broadcasted_iota(jnp.int32, (blocks, cluster), 1)).astype(
        jnp.float32
    )
    pairs = [(0, 0), (0, 1), (0, 2), (1, 1), (1, 2), (2, 2)]
    prods = jnp.stack([jnp.sum(jpt[:, a] * jpt[:, b], axis=0).reshape(-1) for a, b in pairs])
    local_blocks = jnp.zeros((6, PTS), jnp.float32).at[:, flat_ids].add(prods)
    cof = cofactors(lax.psum(local_blocks, "cam"))
    diag_blocks = jnp.sum(jcam * jcam, axis=(0, 3))
    diag_local = jnp.dot(
        diag_blocks, one_hot, precision=highest, preferred_element_type=jnp.float32
    )
    precond = lax.psum_scatter(diag_local, "slab", scatter_dimension=1, tiled=True) + LAMBDA
    solution = jnp.zeros_like(rhs)
    residual = rhs
    precond_res = residual / precond
    direction = precond_res
    rz_now = precond_dot(residual, precond_res)
    for step in range(ITERS):
        gathered = lax.all_gather(direction, "slab", axis=1, tiled=True)
        per_block = lax.dot_general(
            gathered,
            one_hot,
            (((1,), (1,)), ((), ())),
            precision=highest,
            preferred_element_type=jnp.float32,
        )
        errors = jnp.sum(jcam * per_block[None, :, :, None], axis=1)
        pulled = jnp.sum(jpt * errors[:, None], axis=0).reshape(3, -1)
        local_q = jnp.zeros((3, PTS), jnp.float32).at[:, flat_ids].add(pulled)
        summed = lax.psum(local_q, "cam")
        eliminated = solve_points(cof, summed)
        at_slots = jnp.take(eliminated, flat_ids, axis=1).reshape(3, blocks, slots)
        reduced = errors - jnp.sum(jpt * at_slots[None], axis=1)
        block_terms = jnp.sum(jcam * reduced[:, None], axis=(0, 3))
        cluster_terms = jnp.dot(
            block_terms, one_hot, precision=highest, preferred_element_type=jnp.float32
        )
        image = (
            lax.psum_scatter(cluster_terms, "slab", scatter_dimension=1, tiled=True)
            + LAMBDA * direction
        )
        alpha = rz_now / lax.psum(jnp.sum(direction * image), ("slab", "cam"))
        solution = solution + alpha * direction
        residual = residual - alpha * image
        precond_res = residual / precond
        rz_next = precond_dot(residual, precond_res)
        direction = precond_res + rz_next / rz_now * direction
        rz_now = rz_next
    return (solution, residual)


def solution(mesh):
    placed = (
        P(None, ("slab", "cam"), None),
        P(None, ("slab", "cam"), None),
        P(("slab", "cam"), None),
        P(("slab", "cam")),
        P(("slab", "cam")),
        P(None, ("slab", "cam")),
    )
    return jax.shard_map(
        local,
        mesh=mesh,
        in_specs=placed,
        out_specs=(P(None, ("slab", "cam")), P(None, ("slab", "cam"))),
        check_vma=False,
    )
```

profile of v0, /device:TPU:1, one launch (start us, length us, event | category | flops | bytes accessed | tf_op | source)
XLA Modules:
  0.0 1092.4 jit_solution(18149725102360472870)
XLA Ops:
  9.3 3.3 convolution_bitcast_fusion.2
  13.2 2.7 copy.67
  15.8 48.0 %scatter_custom_fusion = f32[6,16384]{0,1:T(8,128)} fusion(s32[8192]{0:T(1024)S(1)} %bitcast.78, f32[8192,6]{1,0:T(8,128)} %copy.67, f32[]{:T(128)} %constant.0.clone.1), kind=kCustom, calls=%fused_computation.9 | custom fusion | flops 49152 | bytes 393728 | tf_op jit(solution)/shard_map/scatter-add | solution.py:58
  63.8 6.1 copy.68
  69.9 81.5 %reduce-scatter.10.cloned.1.call-done = f32[48,9]{1,0:T(8,128)} async-done(((f32[3072,9]{1,0:T(8,128)}), f32[48,9]{1,0:T(8,128)}) %reduce-scatter.10.cloned.1.call-update) | async-done | bytes 1744
  152.3 54.9 %all-gather = f32[64,48,9]{1,2,0:T(8,128)S(1)} all-gather(f32[1,48,9]{1,2,0:T(8,128)S(1)} %fusion.15), channel_id=1, replica_groups=mesh['slab'=64,'cam'=4] {'slab'}, dimensions={0}, use_global_device_ids=true | all-gather | bytes 112320 | tf_op jit(solution)/shard_map/all_gather | solution.py:71
  208.2 2.6 copy.78
  210.9 48.0 %scatter_custom_fusion.1 = f32[3,16384]{0,1:T(8,128)} fusion(s32[8192]{0:T(1024)S(1)} %bitcast.79, f32[8192,3]{1,0:T(8,128)} %bitcast.66, f32[]{:T(128)} %constant.0.clone.1), kind=kCustom, calls=%fused_computation.7 | custom fusion | flops 24576 | bytes 197120 | tf_op jit(solution)/shard_map/scatter-add | solution.py:81
  258.9 5.9 copy.70
  265.1 45.6 %all-reduce.7.cloned.1.call-done = (f32[6,16384]{1,0:T(8,128)}, f32[3,16384]{1,0:T(4,128)}) async-done(((f32[6,16384]{1,0:T(8,128)}, f32[3,16384]{1,0:T(4,128)}), (f32[6,16384]{1,0:T(8,128)}, f32[3,16384]{1,0:T(4,128)})) %all-reduce.7.cloned.1.call-update) | async-done | bytes 589840 | tf_op jit(solution)/shard_map/psum | solution.py:59
  310.7 3.3 add_divide_fusion.5
  314.0 2.8 add_divide_fusion.4
  319.2 5.1 copy.71
  324.2 31.1 %gather_fusion = f32[8192,3]{1,0:T(8,128)} fusion(f32[3,16384]{0,1:T(8,128)} %copy.71, s32[8192]{0:T(1024)S(1)} %fusion.14), kind=kCustom, calls=%fused_computation.clone | custom fusion | bytes 229376 | tf_op jit(solution)/shard_map/jit(_take)/gather | solution.py:84
  355.3 7.4 broadcast_select_fusion.1
  362.8 2.8 copy.72
  366.0 2.6 convolution_bitcast_fusion.1
  368.7 137.8 %reduce-scatter.12.cloned.1.call-done = f32[48,9]{1,0:T(8,128)} async-done(((f32[3072,9]{1,0:T(8,128)}), f32[48,9]{1,0:T(8,128)}) %reduce-scatter.12.cloned.1.call-update) | async-done | bytes 1744
  507.9 79.6 %all-reduce = (f32[]{:T(128)}, f32[]{:T(128)}) all-reduce(f32[]{:T(128)} %get-tuple-element.10, f32[]{:T(128)} %get-tuple-element.9), channel_id=1, replica_groups=mesh['slab'=64,'cam'=4] {'slab','cam'}, use_global_device_ids=true, to_apply=%region_4.0 | all-reduce | flops 2 | bytes 16 | tf_op jit(solution)/shard_map/psum | solution.py:40
  589.5 73.5 %psum.53 = f32[]{:T(128)} all-reduce(f32[]{:T(128)} %multiply_reduce_fusion.16), channel_id=1, replica_groups=mesh['slab'=64,'cam'=4] {'slab','cam'}, use_global_device_ids=true, to_apply=%region_24.26 | all-reduce | flops 1 | bytes 8 | tf_op jit(solution)/shard_map/psum | solution.py:40
  664.4 49.3 %all-gather.1 = f32[64,48,9]{1,2,0:T(8,128)S(1)} all-gather(f32[1,48,9]{1,2,0:T(8,128)S(1)} %bitcast.71), channel_id=1, replica_groups=mesh['slab'=64,'cam'=4] {'slab'}, dimensions={0}, use_global_device_ids=true | all-gather | bytes 112320 | tf_op jit(solution)/shard_map/all_gather | solution.py:71
  714.8 2.6 copy.79
  717.4 48.0 %scatter_custom_fusion.2 = f32[3,16384]{0,1:T(8,128)} fusion(s32[8192]{0:T(1024)S(1)} %bitcast.80, f32[8192,3]{1,0:T(8,128)} %bitcast.65, f32[]{:T(128)} %constant.0.clone.1), kind=kCustom, calls=%fused_computation.5 | custom fusion | flops 24576 | bytes 197120 | tf_op jit(solution)/shard_map/scatter-add | solution.py:81
  765.4 6.0 copy.75
  771.5 40.9 %all-reduce.5.cloned.1.call-done = f32[3,16384]{1,0:T(4,128)} async-done(((f32[3,16384]{1,0:T(4,128)}), f32[3,16384]{1,0:T(4,128)}) %all-reduce.5.cloned.1.call-update) | async-done | bytes 196624 | tf_op jit(solution)/shard_map/psum | solution.py:82
  815.7 5.1 copy.76
  820.8 31.1 %gather_fusion.1 = f32[8192,3]{1,0:T(8,128)} fusion(f32[3,16384]{0,1:T(8,128)} %copy.76, s32[8192]{0:T(1024)S(1)} %fusion.14), kind=kCustom, calls=%fused_computation.1.clone | custom fusion | bytes 229376 | tf_op jit(solution)/shard_map/jit(_take)/gather | solution.py:84
  851.9 7.4 broadcast_select_fusion
  859.3 2.8 copy.77
  862.6 2.6 convolution_bitcast_fusion
  865.2 137.9 %reduce-scatter.14.cloned.1.call-done = f32[48,9]{1,0:T(8,128)} async-done(((f32[3072,9]{1,0:T(8,128)}), f32[48,9]{1,0:T(8,128)}) %reduce-scatter.14.cloned.1.call-update) | async-done | bytes 1744
  1004.5 79.5 %psum.55 = f32[]{:T(128)} all-reduce(f32[]{:T(128)} %multiply_reduce_fusion.15), channel_id=1, replica_groups=mesh['slab'=64,'cam'=4] {'slab','cam'}, use_global_device_ids=true, to_apply=%region_34.36 | all-reduce | flops 1 | bytes 8 | tf_op jit(solution)/shard_map/psum | solution.py:94
  (66 shorter events, 16.3 us)
Async XLA Ops:
  7.2 5.6 copy-start.1
  7.2 5.6 copy-start.3
  7.2 144.3 %reduce-scatter.10.cloned.1.call-start = ((), (), s32[]{:S(2)}) async-start(), calls=%async_computation.4 | async-start | bytes 1597440
  12.7 298.1 %all-reduce.7.cloned.1.call-start = ((), (), s32[]{:S(2)}) async-start(), calls=%async_computation.7 | async-start | bytes 1572864 | tf_op jit(solution)/shard_map/psum | solution.py:59
  63.8 88.4 %copy-start.2 = (f32[9,48]{1,0:T(8,128)S(1)}, f32[9,48]{1,0:T(8,128)}, u32[]{:S(2)}) copy-start(f32[9,48]{1,0:T(8,128)} %param.13) | copy-start | bytes 5188
  63.8 143.6 %copy-start.4 = (s32[64]{0:T(128)S(1)}, s32[64]{0:T(128)}, u32[]{:S(2)}) copy-start(s32[64]{0:T(128)} %param.11) | copy-start | bytes 772
  264.8 241.7 %reduce-scatter.12.cloned.1.call-start = ((), (), s32[]{:S(2)}) async-start(), calls=%async_computation.5 | async-start | bytes 1597440
  368.7 443.7 %all-reduce.5.cloned.1.call-start = ((), (), s32[]{:S(2)}) async-start(), calls=%async_computation.3 | async-start | bytes 524288 | tf_op jit(solution)/shard_map/psum | solution.py:82
  765.4 46.9 %copy-start = (f32[6,16384]{1,0:T(8,128)S(1)}, f32[6,16384]{1,0:T(8,128)}, u32[]{:S(2)}) copy-start(f32[6,16384]{1,0:T(8,128)} %get-tuple-element.13) | copy-start | bytes 1179652
  771.4 231.7 %reduce-scatter.14.cloned.1.call-start = ((), (), s32[]{:S(2)}) async-start(), calls=%async_computation.6 | async-start | bytes 1597440
Sparse Core Ops, SparseCore 0:
  12.8 138.6 reduce-scatter.9
  265.0 45.7 all-reduce.6
  368.8 137.6 reduce-scatter.11
  771.5 40.7 all-reduce.4
  865.3 137.6 reduce-scatter.13
where the time goes:
time: 1090 us
  waiting for transfers between devices  444 us (41%)
  blocking collectives  337 us (31%)
  other arithmetic  176 us (16%)
  local copies, waits for them, and re-layouts  107 us (10%)
  between operations  18.1 us (2%)
    unnamed x8, waiting for transfers between devices  357 us
    psum x2, blocking collectives, precond_dot(): return lax.psum(jnp.sum(residual * precond_res), ('slab', 'cam'))  153 us
    all_gather x2, blocking collectives, local(): gathered = lax.all_gather(direction, 'slab', axis=1, tiled=True)  104 us
    scatter-add x2, other arithmetic, local(): local_q = jnp.zeros((3, PTS), jnp.float32).at[:, flat_ids].add(pulled)  96 us
    psum x1, blocking collectives, local(): alpha = rz_now / lax.psum(jnp.sum(direction * image), ('slab', 'cam'))  79.5 us
    gather x2, local copies, waits for them, and re-layouts, local(): at_slots = jnp.take(eliminated, flat_ids, axis=1).reshape(3, blocks, slots)  62.2 us
    scatter-add x1, other arithmetic, local(): local_blocks = jnp.zeros((6, PTS), jnp.float32).at[:, flat_ids].add(prods)  48 us
    psum x1, waiting for transfers between devices, local(): cof = cofactors(lax.psum(local_blocks, 'cam'))  45.6 us
  transfers between devices with their start and end apart: 5, of which 5 were waited for; matrix products, arithmetic and copies ran while one was open for 5% of the time, Pallas kernels for 0%

commit v1 on v0

v1 whole, which is shorter than its diff:
```python
import jax
import jax.numpy as jnp
from jax import lax
from jax.experimental import pallas as pl
from jax.experimental.pallas import tpu as pltpu
from jax.sharding import PartitionSpec as P

MU = 1.0
LAMBDA = 0.5

MESH = pl.DeviceIdType.MESH
F32 = jnp.float32
BF16 = jnp.bfloat16

BLK = 64
SLOTS = 128
OWN = 48
NZ = 8
NG = 8
NCAM = 4
HI = 256
LO = 64
LQ = LO // NCAM
CHUNK = 256
CHUNKS = BLK * SLOTS // CHUNK
ROWS = 10

NT = (((1,), (1,)), ((), ()))


def dot_nt(a, b):
    return lax.dot_general(a, b, NT, preferred_element_type=F32)


def dot_nn(a, b):
    return lax.dot_general(a, b, (((1,), (0,)), ((), ())), preferred_element_type=F32)


def split2(v):
    hi = v.astype(BF16).astype(F32)
    return hi, v - hi


def split3(v):
    hi, rest = split2(v)
    mid, low = split2(rest)
    return hi, mid, low


def slab_of(x, z, core):
    return x * (NZ * 2) + z * 2 + core


def total(v):
    return jnp.sum(jnp.sum(v, axis=0, keepdims=True), axis=1, keepdims=True)


def kernel(
    jc_ref, jp_ref, pid_ref, cam_ref, fill_ref, rhs_ref, sol_ref, res_ref,
    jcm, jpm, low_b, low_f, high, equal, t_ref, w_obs, e_ref,
    v_part, v_recv, cof, q_part, q_recv, w_full, w_split, xz, xg, sc,
    zs, zr, gs, gr, vs, vr, qs, qr, ws, wr, ss, sr,
):
    slab = lax.axis_index("slab")
    cam = lax.axis_index("cam")
    core = lax.rem(slab, 2)
    z = lax.rem(lax.div(slab, 2), NZ)
    x = lax.div(slab, 2 * NZ)
    g = x * 2 + core
    odd = lax.rem(z, 2)

    def z_peer(d):
        return (slab_of(x, lax.rem(z + d, NZ), core), cam)

    def g_peer(d):
        other = lax.rem(g + d, NG)
        return (slab_of(lax.div(other, 2), z, lax.rem(other, 2)), cam)

    def cam_peer(d):
        return (slab, lax.rem(cam + d, NCAM))

    barrier = pltpu.get_barrier_semaphore()
    for d in range(1, NZ):
        pl.semaphore_signal(barrier, inc=1, device_id=z_peer(d), device_id_type=MESH)
    for d in range(1, NG):
        pl.semaphore_signal(barrier, inc=1, device_id=g_peer(d), device_id_type=MESH)
    for d in range(1, NCAM):
        pl.semaphore_signal(barrier, inc=1, device_id=cam_peer(d), device_id_type=MESH)
    pl.semaphore_wait(barrier, NZ - 1 + NG - 1 + NCAM - 1)

    pending = []

    def remote(src, dst, send, recv, device):
        copy = pltpu.make_async_remote_copy(
            src_ref=src, dst_ref=dst, send_sem=send, recv_sem=recv, device_id=device, device_id_type=MESH
        )
        copy.start()
        pending.append(copy)
        return copy

    def wait_all(copies):
        for copy in copies:
            copy.wait_recv()

    def z_start(m):
        return [
            remote(xz.at[m, z], xz.at[m, z], zs.at[m, d - 1], zr.at[m, d - 1], z_peer(d))
            for d in range(1, NZ)
        ]

    def g_start(m):
        for p in range(NZ // 2):
            xg[m, g, ROWS * p : ROWS * (p + 1), :] = xz[m, 2 * p] + xz[m, 2 * p + 1]
        return [
            remote(xg.at[m, g], xg.at[m, g], gs.at[m, d - 1], gr.at[m, d - 1], g_peer(d))
            for d in range(1, NG)
        ]

    def camera_sums(m, matrix):
        acc = jnp.zeros((128, 48), F32)
        for other in range(NG):
            rows = xg[m, other]
            wide = jnp.concatenate([rows[ROWS * p : ROWS * (p + 1)] for p in range(NZ // 2)], axis=1)
            wide = jnp.concatenate([wide, jnp.zeros((16 - ROWS, 512), F32)], axis=0)
            parts = jnp.concatenate(split3(wide), axis=0).astype(BF16)
            acc = acc + dot_nt(matrix(other), parts)
        return acc[:, 0:16] + acc[:, 16:32] + acc[:, 32:48]

    rhs = rhs_ref[...]
    first = jnp.concatenate([rhs, jnp.zeros((9, 128 - OWN), F32)], axis=1)
    second = jnp.concatenate([jnp.zeros((9, 64), F32), rhs, jnp.zeros((9, 64 - OWN), F32)], axis=1)
    placed = jnp.where(odd == 0, first, second)
    xz[1, z] = jnp.concatenate([placed, jnp.zeros((1, 128), F32)], axis=0)
    rhs_z = z_start(1)

    def column(row):
        wide = jnp.concatenate([row, jnp.zeros((1, 64), F32)], axis=1)
        return jnp.broadcast_to(wide, (128, 128)).T

    cam_col = column(cam_ref[...].astype(F32))
    fill_col = column(fill_ref[...].astype(F32))
    sub = lax.broadcasted_iota(jnp.int32, (128, 128), 0)
    lane = lax.broadcasted_iota(jnp.int32, (128, 128), 1)
    own_cam = (slab * OWN + sub - 64).astype(F32)
    is_own = (sub >= 64) & (sub < 64 + OWN)
    targets = jnp.where(sub < 64, cam_col, jnp.where(is_own, own_cam, -1.0))

    live = (lane.astype(F32) < fill_col)[:BLK]
    for i in range(18):
        jcm[i] = jnp.where(live, jc_ref[i], 0.0)
    for i in range(6):
        jpm[i] = jnp.where(live, jp_ref[i], 0.0)

    lane64 = lane[:BLK]
    sub64 = sub[:BLK]

    def to_message(m, columns):
        padded = jnp.zeros((64, 128), F32)
        both = jnp.where(
            odd == 0,
            jnp.concatenate([columns, padded], axis=0),
            jnp.concatenate([padded, columns], axis=0),
        )
        xz[m, z] = both.T[:ROWS]

    diag = jnp.where(lane64 == 9, cam_col[:BLK], 0.0)
    for j in range(9):
        square = jnp.sum(jcm[j] * jcm[j] + jcm[9 + j] * jcm[9 + j], axis=1, keepdims=True)
        diag = jnp.where(lane64 == j, square, diag)
    to_message(0, diag)
    diag_z = z_start(0)

    def build(k, carry):
        ids = jnp.concatenate([pid_ref[pl.ds(2 * k, 1), :], pid_ref[pl.ds(2 * k + 1, 1), :]], axis=1)
        low = lax.bitwise_and(ids, LO - 1)
        top = lax.shift_right_logical(ids, 6)
        hot = lax.broadcasted_iota(jnp.int32, (HI, CHUNK), 0) == top
        high[k] = jnp.where(hot, 1.0, 0.0).astype(BF16)
        hot_low = jnp.where(lax.broadcasted_iota(jnp.int32, (LO, CHUNK), 0) == low, 1.0, 0.0)
        low_f[k] = hot_low
        low_b[k] = hot_low.astype(BF16)
        return carry

    lax.fori_loop(0, CHUNKS, build, 0)

    wait_all(rhs_z)
    rhs_g = g_start(1)
    wait_all(diag_z)
    diag_g = g_start(0)

    def pair(ref, index, k):
        return jnp.concatenate([ref[index, pl.ds(2 * k, 1), :], ref[index, pl.ds(2 * k + 1, 1), :]], axis=1)

    def scatter(rows_of, count, acc_ref):
        half = NCAM * count * LQ
        acc_ref[...] = jnp.zeros_like(acc_ref)

        def body(k, carry):
            parts = [], []
            for row in rows_of(k):
                for part, value in zip(parts, split2(row)):
                    part.append(jnp.broadcast_to(value, (LQ, CHUNK)).astype(BF16))
            blocks = [
                low_b[k, LQ * q : LQ * (q + 1), :] * value for part in parts for q in range(NCAM) for value in part
            ]
            product = dot_nt(jnp.concatenate(blocks, axis=0), high[k])
            acc_ref[...] += (product[:half] + product[half:]).reshape(NCAM, count * LQ, HI)
            return carry

        lax.fori_loop(0, CHUNKS, body, 0)

    def jp_products(k):
        a = [pair(jpm, i, k) for i in range(6)]
        return [a[i] * a[j] + a[3 + i] * a[3 + j] for i, j in ((0, 0), (0, 1), (0, 2), (1, 1), (1, 2), (2, 2))]

    scatter(jp_products, 6, v_part)
    v_copies = [
        remote(v_part.at[lax.rem(cam + d, NCAM)], v_recv.at[d - 1], vs.at[d - 1], vr.at[d - 1], cam_peer(d))
        for d in range(1, NCAM)
    ]

    wait_all(diag_g)
    for other in range(NG):
        for p in range(NZ // 2):
            ids = xg[0, other, ROWS * p + 9 : ROWS * p + 10, :]
            equal[other, :, 128 * p : 128 * (p + 1)] = jnp.where(targets == ids, 1.0, 0.0).astype(BF16)

    def same(other):
        return equal[other]

    def owned(other):
        lanes = lax.broadcasted_iota(jnp.int32, (1, 128), 1)
        place = lax.rem(lanes, 64)
        blocks = []
        for p in range(NZ // 2):
            source = (other // 2) * (2 * NZ) + (2 * p + lax.div(lanes, 64)) * 2 + other % 2
            ids = jnp.where(place < OWN, source * OWN + place, -2).astype(F32)
            blocks.append(jnp.where(targets == ids, 1.0, 0.0).astype(BF16))
        return jnp.concatenate(blocks, axis=1)

    lane16 = lax.broadcasted_iota(jnp.int32, (128, 16), 1)
    sub16 = lax.broadcasted_iota(jnp.int32, (128, 16), 0)
    param = lane16 < 9
    mine = param & (sub16 >= 64) & (sub16 < 64 + OWN)
    precond = jnp.where(param, camera_sums(0, same), 0.0) + LAMBDA
    wait_all(rhs_g)
    res0 = camera_sums(1, owned)
    dir0 = res0 / precond

    def apply(it, vec, scalars):
        cols = [jnp.broadcast_to(vec[:BLK, j : j + 1], (BLK, SLOTS)) for j in range(9)]
        for r in range(2):
            e = jcm[9 * r] * cols[0]
            for j in range(1, 9):
                e = e + jcm[9 * r + j] * cols[j]
            e_ref[r] = e
        for a in range(3):
            t_ref[a] = jpm[a] * e_ref[0] + jpm[3 + a] * e_ref[1]
        scatter(lambda k: [pair(t_ref, a, k) for a in range(3)], 3, q_part.at[it])
        q_copies = [
            remote(
                q_part.at[it, lax.rem(cam + d, NCAM)], q_recv.at[it, d - 1],
                qs.at[it, d - 1], qr.at[it, d - 1], cam_peer(d),
            )
            for d in range(1, NCAM)
        ]
        if it == 0:
            wait_all(v_copies)
            v = v_part[cam] + v_recv[0] + v_recv[1] + v_recv[2]
            v00, v01, v02, v11, v12, v22 = [v[LQ * i : LQ * (i + 1)] for i in range(6)]
            v00, v11, v22 = v00 + MU, v11 + MU, v22 + MU
            c00 = v11 * v22 - v12 * v12
            c01 = v02 * v12 - v01 * v22
            c02 = v01 * v12 - v02 * v11
            c11 = v00 * v22 - v02 * v02
            c12 = v01 * v02 - v00 * v12
            c22 = v00 * v11 - v01 * v01
            det = v00 * c00 + v01 * c01 + v02 * c02
            for i, value in enumerate((c00, c01, c02, c11, c12, c22)):
                cof[i] = value
            cof[6] = det
        wait_all(q_copies)
        q = q_part[it, cam] + q_recv[it, 0] + q_recv[it, 1] + q_recv[it, 2]
        q0, q1, q2 = [q[LQ * i : LQ * (i + 1)] for i in range(3)]
        det = cof[6]
        w0 = (cof[0] * q0 + cof[1] * q1 + cof[2] * q2) / det
        w1 = (cof[1] * q0 + cof[3] * q1 + cof[4] * q2) / det
        w2 = (cof[2] * q0 + cof[4] * q1 + cof[5] * q2) / det
        w_full[it, cam] = jnp.concatenate([w0, w1, w2], axis=0)
        w_copies = [
            remote(w_full.at[it, cam], w_full.at[it, cam], ws.at[it, d - 1], wr.at[it, d - 1], cam_peer(d))
            for d in range(1, NCAM)
        ]
        wait_all(w_copies)
        half = NCAM * 3 * LQ
        for part, value in enumerate(split2(w_full[it].reshape(half, HI))):
            w_split[half * part : half * (part + 1)] = value.astype(BF16)

        def body(k, carry):
            product = dot_nn(w_split[...], high[k])
            product = product[:half] + product[half:]
            for c in range(3):
                picked = jnp.zeros((LQ, CHUNK), F32)
                for q in range(NCAM):
                    at = (3 * q + c) * LQ
                    picked = picked + product[at : at + LQ] * low_f[k, LQ * q : LQ * (q + 1), :]
                row = jnp.sum(picked, axis=0, keepdims=True)
                w_obs[c, pl.ds(2 * k, 1), :] = row[:, :SLOTS]
                w_obs[c, pl.ds(2 * k + 1, 1), :] = row[:, SLOTS:]
            return carry

        lax.fori_loop(0, CHUNKS, body, 0)
        d = [
            e_ref[r] - (jpm[3 * r] * w_obs[0] + jpm[3 * r + 1] * w_obs[1] + jpm[3 * r + 2] * w_obs[2])
            for r in range(2)
        ]
        terms = jnp.zeros((BLK, 128), F32)
        for j in range(9):
            term = jnp.sum(jcm[j] * d[0] + jcm[9 + j] * d[1], axis=1, keepdims=True)
            terms = jnp.where(lane64 == j, term, terms)
        if scalars is not None:
            known = scalars + [LAMBDA * total(jnp.where(mine, vec * vec, 0.0)) + total(terms[:, :16] * vec[:BLK])]
            for i, value in enumerate(known):
                terms = jnp.where((lane64 == 9) & (sub64 == i), value, terms)
        m = 2 + it
        to_message(m, terms)
        wait_all(z_start(m))
        wait_all(g_start(m))
        return m

    m = apply(0, dir0, None)
    image0 = jnp.where(param, camera_sums(m, same), 0.0) + LAMBDA * dir0
    rest = res0 - image0
    dir1 = rest / precond
    dots = [total(jnp.where(mine, a * b, 0.0)) for a, b in ((res0, dir0), (dir0, rest), (rest, dir1))]
    m = apply(1, dir1, dots)

    row = jnp.zeros((1, 128), F32)
    for other in range(NG):
        for p in range(NZ // 2):
            row = row + xg[m, other, ROWS * p + 9 : ROWS * p + 10, :]
    row = row[:, :64] + row[:, 64:]
    sc[cam] = jnp.concatenate([row, jnp.zeros((1, 64), F32)], axis=1)
    sc_copies = [
        remote(sc.at[cam], sc.at[cam], ss.at[d - 1], sr.at[d - 1], cam_peer(d)) for d in range(1, NCAM)
    ]
    image1 = jnp.where(param, camera_sums(m, same), 0.0) + LAMBDA * dir1
    wait_all(sc_copies)
    sums = sc[0] + sc[1] + sc[2] + sc[3]
    aa, bb, cc, dd = [sums[:, i : i + 1] for i in range(4)]
    curve = aa - bb
    alpha0 = aa / curve
    keep = -bb / curve
    rz1 = keep * keep * aa + 2.0 * keep * alpha0 * bb + alpha0 * alpha0 * cc
    scale = keep + rz1 / aa
    alpha1 = rz1 / (scale * scale * curve + 2.0 * scale * alpha0 * (bb - cc) + alpha0 * alpha0 * dd)
    dir_last = scale * dir0 + alpha0 * dir1
    img_last = scale * image0 + alpha0 * image1
    sol = alpha0 * dir0 + alpha1 * dir_last
    res = keep * res0 + alpha0 * rest - alpha1 * img_last

    def to_rows(value):
        wide = jnp.concatenate([value, jnp.zeros((128, 112), F32)], axis=1)
        return wide.T[:9, 64 : 64 + OWN]

    sol_ref[...] = to_rows(sol)
    res_ref[...] = to_rows(res)
    for copy in pending:
        copy.wait_send()


def local(jac_cam, jac_point, point_ids, block_cam, block_fill, rhs):
    dma = pltpu.SemaphoreType.DMA
    vmem = pl.BlockSpec(memory_space=pltpu.VMEM)
    own = jax.ShapeDtypeStruct((9, OWN), F32)
    return pl.pallas_call(
        kernel,
        out_shape=(own, own),
        in_specs=[vmem] * 6,
        out_specs=(vmem, vmem),
        scratch_shapes=[
            pltpu.VMEM((18, BLK, SLOTS), F32),
            pltpu.VMEM((6, BLK, SLOTS), F32),
            pltpu.VMEM((CHUNKS, LO, CHUNK), BF16),
            pltpu.VMEM((CHUNKS, LO, CHUNK), F32),
            pltpu.VMEM((CHUNKS, HI, CHUNK), BF16),
            pltpu.VMEM((NG, 128, 512), BF16),
            pltpu.VMEM((3, BLK, SLOTS), F32),
            pltpu.VMEM((3, BLK, SLOTS), F32),
            pltpu.VMEM((2, BLK, SLOTS), F32),
            pltpu.VMEM((NCAM, 6 * LQ, HI), F32),
            pltpu.VMEM((NCAM - 1, 6 * LQ, HI), F32),
            pltpu.VMEM((7, LQ, HI), F32),
            pltpu.VMEM((2, NCAM, 3 * LQ, HI), F32),
            pltpu.VMEM((2, NCAM - 1, 3 * LQ, HI), F32),
            pltpu.VMEM((2, NCAM, 3 * LQ, HI), F32),
            pltpu.VMEM((2 * NCAM * 3 * LQ, HI), BF16),
            pltpu.VMEM((4, NZ, ROWS, 128), F32),
            pltpu.VMEM((4, NG, ROWS * NZ // 2, 128), F32),
            pltpu.VMEM((NCAM, 1, 128), F32),
            dma((4, NZ - 1)),
            dma((4, NZ - 1)),
            dma((4, NG - 1)),
            dma((4, NG - 1)),
            dma((NCAM - 1,)),
            dma((NCAM - 1,)),
            dma((2, NCAM - 1)),
            dma((2, NCAM - 1)),
            dma((2, NCAM - 1)),
            dma((2, NCAM - 1)),
            dma((NCAM - 1,)),
            dma((NCAM - 1,)),
        ],
        compiler_params=pltpu.CompilerParams(
            collective_id=0, has_side_effects=True, vmem_limit_bytes=40 * 1024 * 1024
        ),
        name="schur_cg",
    )(jac_cam, jac_point, point_ids, block_cam.reshape(1, BLK), block_fill.reshape(1, BLK), rhs)


def solution(mesh):
    placed = (
        P(None, ("slab", "cam"), None),
        P(None, ("slab", "cam"), None),
        P(("slab", "cam"), None),
        P(("slab", "cam")),
        P(("slab", "cam")),
        P(None, ("slab", "cam")),
    )
    return jax.shard_map(
        local,
        mesh=mesh,
        in_specs=placed,
        out_specs=(P(None, ("slab", "cam")), P(None, ("slab", "cam"))),
        check_vma=False,
    )
```

time: 1090 us -> 104 us (0.10)
  waiting for transfers between devices: 444 us -> 0 us
  blocking collectives: 337 us -> 0 us
  other arithmetic: 176 us -> 0 us
  local copies, waits for them, and re-layouts: 107 us -> 5.3 us
  Pallas kernels: 0 us -> 97.7 us
  between operations: 18.1 us -> 0.66 us
    unnamed x8 -> x0, waiting for transfers between devices: 357 us -> none
    psum x3 -> x0, blocking collectives: 233 us -> none  [the longest x2 153 us: precond_dot(): return lax.psum(jnp.sum(residual * precond_res), ('slab', 'cam'))]
    scatter-add x3 -> x0, other arithmetic: 144 us -> none  [the longest x2 96 us: local(): local_q = jnp.zeros((3, PTS), jnp.float32).at[:, flat_ids].add(pulled)]
    all_gather x2 -> x0, blocking collectives: 104 us -> none  [local(): gathered = lax.all_gather(direction, 'slab', axis=1, tiled=True)]
    pallas_call x0 -> x1, Pallas kernels: none -> 97.7 us  [local(): pl.pallas_call(kernel, out_shape=(own, own), in_specs=[vmem] * 6, out_spe...]
    psum x2 -> x0, waiting for transfers between devices: 86.5 us -> none  [the longest x1 45.6 us: local(): cof = cofactors(lax.psum(local_blocks, 'cam'))]
    gather x2 -> x0, local copies, waits for them, and re-layouts: 62.2 us -> none  [local(): at_slots = jnp.take(eliminated, flat_ids, axis=1).reshape(3, blocks, slots)]
    scatter-add x3 -> x0, local copies, waits for them, and re-layouts: 18 us -> none  [the longest x2 11.9 us: local(): local_q = jnp.zeros((3, PTS), jnp.float32).at[:, flat_ids].add(pulled)]
  transfers between devices with their start and end apart: 5 -> 0, of which waited for: 5 -> 0; matrix products, arithmetic and copies ran while one was open for 5% -> 0% of each run, Pallas kernels for 0% -> 0%
where the time goes in v1:
time: 104 us
  Pallas kernels  97.7 us (94%)
  local copies, waits for them, and re-layouts  5.3 us (5%)
    pallas_call x1, Pallas kernels, local(): pl.pallas_call(kernel, out_shape=(own, own), in_specs=[vmem] * 6, out_spe...  97.7 us
    unnamed x14, local copies, waits for them, and re-layouts  5.3 us

profile of v1, /device:TPU:1, one launch (start us, length us, event | category | flops | bytes accessed | tf_op | source)
XLA Modules:
  0.0 103.6 jit_solution(15249422277500649746)
XLA Ops:
  0.6 0.0 copy-start.4
  0.6 0.0 copy-start.5
  0.7 0.6 copy-done.4
  1.3 0.0 copy-done.5
  1.3 0.0 copy-start
  1.3 1.1 %copy-done = f32[18,64,128]{2,1,0:T(8,128)S(1)} copy-done((f32[18,64,128]{2,1,0:T(8,128)S(1)}, f32[18,64,128]{2,1,0:T(8,128)}, u32[]{:S(2)}) %copy-start) | copy-done | bytes 589848
  2.4 0.0 copy-start.1
  2.4 0.9 copy-done.1
  3.3 0.0 copy-start.2
  3.3 0.8 copy-done.2
  4.1 0.0 copy-start.3
  4.1 0.7 copy-done.3
  4.8 97.7 %schur_cg.1 = (f32[9,48]{1,0:T(8,128)S(1)}, f32[9,48]{1,0:T(8,128)S(1)}) custom-call(f32[18,64,128]{2,1,0:T(8,128)S(1)} %copy-done, f32[6,64,128]{2,1,0:T(8,128)S(1)} %copy-done.1, s32[64,128]{1,0:T(8,128)S(1)} %copy-done.2, s32[1,64]{1,0:T(1,128)S(1)} %bitcast.2, s32[1,64]{1,0:T(1,128)S(1)} %bitcast.3, f32[9,48]{1,0:T(8,128)S(1)} %copy-done.3), custom_call_target="tpu_custom_call" | custom-call | tf_op jit(solution)/shard_map/schur_cg/pallas_call | solution.py:376
  102.4 0.6 copy.10
  103.0 0.6 copy.11
Async XLA Ops:
  0.6 0.7 copy-start.4
  0.6 0.7 copy-start.5
  1.3 1.1 %copy-start = (f32[18,64,128]{2,1,0:T(8,128)S(1)}, f32[18,64,128]{2,1,0:T(8,128)}, u32[]{:S(2)}) copy-start(f32[18,64,128]{2,1,0:T(8,128)} %jc_ref.1) | copy-start | bytes 1769476
  2.4 0.9 copy-start.1
  3.3 0.8 copy-start.2
  4.1 0.7 copy-start.3

commit v2 on v1

v2 whole, which is shorter than its diff:
```python
import jax
import jax.numpy as jnp
from jax import lax
from jax.experimental import pallas as pl
from jax.experimental.pallas import tpu as pltpu
from jax.sharding import PartitionSpec as P

MU = 1.0
LAMBDA = 0.5

MESH = pl.DeviceIdType.MESH
F32 = jnp.float32
BF16 = jnp.bfloat16

BLK = 64
SLOTS = 128
OWN = 48
NX = 4
NZ = 8
NCHIP = NX * NZ
NCAM = 4
HI = 256
LO = 64
LQ = LO // NCAM
CHUNK = 256
CHUNKS = BLK * SLOTS // CHUNK
STEPS = 8
MSG = 5
GROUP = 4

NT = (((1,), (1,)), ((), ()))


def dot_nt(a, b):
    return lax.dot_general(a, b, NT, preferred_element_type=F32)


def dot_nn(a, b):
    return lax.dot_general(a, b, (((1,), (0,)), ((), ())), preferred_element_type=F32)


def split2(v):
    hi = v.astype(BF16).astype(F32)
    return hi, v - hi


def split3(v):
    hi, rest = split2(v)
    mid, low = split2(rest)
    return hi, mid, low


def far_first():
    def hops(offset):
        dx, dz = offset
        return min(dx, NX - dx) + min(dz, NZ - dz)

    offsets = [(dx, dz) for dx in range(NX) for dz in range(NZ) if dx or dz]
    return sorted(offsets, key=hops, reverse=True)


OFFSETS = far_first()


def column_of(j):
    return (j % 2) * 8 + j // 2


def total(v):
    return jnp.sum(jnp.sum(v, axis=0, keepdims=True), axis=1, keepdims=True)


def kernel(
    jc_hbm, jp_hbm, pid_hbm, cam_hbm, fill_hbm, rhs_hbm, sol_ref, res_ref,
    jcm, jpm, pid_ref, cam_ref, fill_ref, rhs_ref, low_b, low_f, high, equal, t_ref, w_obs, e_ref,
    v_part, v_recv, cof, q_part, q_recv, w_full, w_split, first_msg, msgs, sc,
    ins, cs, cr, ps, pr, vs, vr, qs, qr, ws, wr, ss, sr,
):
    slab = lax.axis_index("slab")
    cam = lax.axis_index("cam")
    core = lax.rem(slab, 2)
    z = lax.rem(lax.div(slab, 2), NZ)
    x = lax.div(slab, 2 * NZ)
    chip = x * NZ + z

    def chip_peer(offset):
        dx, dz = offset
        other = lax.rem(x + dx, NX) * NZ + lax.rem(z + dz, NZ)
        return (other * 2 + core, cam)

    sibling = (chip * 2 + (1 - core), cam)

    def cam_peer(d):
        return (slab, lax.rem(cam + d, NCAM))

    inputs = [
        pltpu.make_async_copy(src, dst, ins.at[i])
        for i, (src, dst) in enumerate(
            (
                (fill_hbm, fill_ref), (cam_hbm, cam_ref), (rhs_hbm, rhs_ref),
                (jc_hbm, jcm), (pid_hbm, pid_ref), (jp_hbm, jpm),
            )
        )
    ]
    for copy in inputs:
        copy.start()
    barrier = pltpu.get_barrier_semaphore()
    for offset in OFFSETS:
        pl.semaphore_signal(barrier, inc=1, device_id=chip_peer(offset), device_id_type=MESH)
    for d in range(1, NCAM):
        pl.semaphore_signal(barrier, inc=1, device_id=cam_peer(d), device_id_type=MESH)
    pl.semaphore_signal(barrier, inc=1, device_id=sibling, device_id_type=MESH)

    pending = []

    def remote(src, dst, send, recv, device):
        copy = pltpu.make_async_remote_copy(
            src_ref=src, dst_ref=dst, send_sem=send, recv_sem=recv, device_id=device, device_id_type=MESH
        )
        copy.start()
        pending.append(copy)
        return copy

    def wait_all(copies):
        for copy in copies:
            copy.wait_recv()

    def gather_start(buf, m):
        mine = buf.at[core, chip]
        return [
            remote(mine, mine, cs.at[m, i], cr.at[m, i], chip_peer(offset)) for i, offset in enumerate(OFFSETS)
        ]

    def gather_end(copies, buf, m):
        wait_all(copies)
        remote(buf.at[core], buf.at[core], ps.at[m], pr.at[m], sibling).wait_recv()

    lane8 = lax.broadcasted_iota(jnp.int32, (8, 128), 1)

    def both_cores(zero, one):
        zero, one = [jnp.concatenate([v, jnp.zeros((8 - MSG, 128), F32)], axis=0) for v in (zero, one)]
        even = jnp.where(lane8 < 64, zero, pltpu.roll(one, 64, 1))
        odd = jnp.where(lane8 < 64, pltpu.roll(zero, 64, 1), one)
        return jnp.concatenate([even, odd], axis=0)

    def camera_sums(read, matrix):
        acc = jnp.zeros((128, 48), F32)
        for group in range(NCHIP // GROUP):
            wide = jnp.concatenate([both_cores(*read(GROUP * group + p)) for p in range(GROUP)], axis=1)
            parts = jnp.concatenate(split3(wide), axis=0).astype(BF16)
            acc = acc + dot_nt(matrix(group), parts)
        return acc[:, 0:16] + acc[:, 16:32] + acc[:, 32:48]

    def column(row):
        wide = jnp.concatenate([row, jnp.zeros((1, 64), F32)], axis=1)
        return jnp.broadcast_to(wide, (128, 128)).T

    for copy in inputs[:4]:
        copy.wait()
    cam_col = column(cam_ref[...].astype(F32))
    fill_col = column(fill_ref[...].astype(F32))
    sub = lax.broadcasted_iota(jnp.int32, (128, 128), 0)
    lane = lax.broadcasted_iota(jnp.int32, (128, 128), 1)
    own_cam = (slab * OWN + sub - 64).astype(F32)
    is_own = (sub >= 64) & (sub < 64 + OWN)
    targets = jnp.where(sub < 64, cam_col, jnp.where(is_own, own_cam, -1.0))

    live = (lane.astype(F32) < fill_col)[:BLK]
    for i in range(18):
        jcm[i] = jnp.where(live, jcm[i], 0.0)

    lane64 = lane[:BLK]
    sub64 = sub[:BLK]

    def spread(values):
        halves = []
        for rest in range(2):
            half = jnp.zeros((BLK, 128), F32)
            for j in range(rest, 9, 2):
                half = jnp.where(lane64 == j // 2, values[j], half)
            halves.append(half)
        return halves

    def message(even, odd):
        return jnp.concatenate([even, odd], axis=0).T[:MSG]

    even, odd = spread(
        [jnp.sum(jcm[j] * jcm[j] + jcm[9 + j] * jcm[9 + j], axis=1, keepdims=True) for j in range(9)]
    )
    odd = jnp.where(lane64 == 4, cam_col[:BLK], odd)
    rhs = rhs_ref[...]
    gap = jnp.zeros((MSG, 64 - OWN), F32)
    none = jnp.zeros((1, OWN), F32)
    rhs_even = jnp.concatenate([rhs[j : j + 1] for j in range(0, 9, 2)], axis=0)
    rhs_odd = jnp.concatenate([rhs[j : j + 1] for j in range(1, 9, 2)] + [none], axis=0)
    first_msg[core, chip] = jnp.concatenate(
        [message(even, odd), jnp.concatenate([rhs_even, gap, rhs_odd, gap], axis=1)], axis=0
    )

    inputs[4].wait()

    def build(k, carry):
        ids = jnp.concatenate([pid_ref[pl.ds(2 * k, 1), :], pid_ref[pl.ds(2 * k + 1, 1), :]], axis=1)
        low = lax.bitwise_and(ids, LO - 1)
        top = lax.shift_right_logical(ids, 6)
        hot = lax.broadcasted_iota(jnp.int32, (HI, CHUNK), 0) == top
        high[k] = jnp.where(hot, 1.0, 0.0).astype(BF16)
        hot_low = jnp.where(lax.broadcasted_iota(jnp.int32, (LO, CHUNK), 0) == low, 1.0, 0.0)
        low_f[k] = hot_low
        low_b[k] = hot_low.astype(BF16)
        return carry

    lax.fori_loop(0, CHUNKS, build, 0)
    inputs[5].wait()
    for i in range(6):
        jpm[i] = jnp.where(live, jpm[i], 0.0)

    pl.semaphore_wait(barrier, len(OFFSETS) + NCAM)
    first_copies = gather_start(first_msg, 0)

    def pair(ref, index, k):
        return jnp.concatenate([ref[index, pl.ds(2 * k, 1), :], ref[index, pl.ds(2 * k + 1, 1), :]], axis=1)

    def scatter(rows_of, count, acc_ref):
        half = NCAM * count * LQ
        acc_ref[...] = jnp.zeros_like(acc_ref)

        def body(step, carry):
            summed = None
            for u in range(STEPS):
                k = step * STEPS + u
                parts = [], []
                for row in rows_of(k):
                    for part, value in zip(parts, split2(row)):
                        part.append(jnp.broadcast_to(value, (LQ, CHUNK)).astype(BF16))
                blocks = [
                    low_b[k, LQ * q : LQ * (q + 1), :] * value
                    for part in parts
                    for q in range(NCAM)
                    for value in part
                ]
                product = dot_nt(jnp.concatenate(blocks, axis=0), high[k])
                summed = product if summed is None else summed + product
            acc_ref[...] += (summed[:half] + summed[half:]).reshape(NCAM, count * LQ, HI)
            return carry

        lax.fori_loop(0, CHUNKS // STEPS, body, 0)

    def jp_products(k):
        a = [pair(jpm, i, k) for i in range(6)]
        return [a[i] * a[j] + a[3 + i] * a[3 + j] for i, j in ((0, 0), (0, 1), (0, 2), (1, 1), (1, 2), (2, 2))]

    scatter(jp_products, 6, v_part)
    v_copies = [
        remote(v_part.at[lax.rem(cam + d, NCAM)], v_recv.at[d - 1], vs.at[d - 1], vr.at[d - 1], cam_peer(d))
        for d in range(1, NCAM)
    ]

    gather_end(first_copies, first_msg, 0)
    lane1 = lax.broadcasted_iota(jnp.int32, (1, 128), 1)

    def same(group):
        blocks = []
        for p in range(GROUP):
            zero, one = [first_msg[c, GROUP * group + p, MSG - 1 : MSG, :] for c in range(2)]
            ids = jnp.where(lane1 < 64, pltpu.roll(zero, 64, 1), one)
            blocks.append(jnp.where(targets == ids, 1.0, 0.0).astype(BF16))
        matrix = jnp.concatenate(blocks, axis=1)
        equal[group] = matrix
        return matrix

    def owned(group):
        place = lax.rem(lane1, 64)
        blocks = []
        for p in range(GROUP):
            source = (GROUP * group + p) * 2 + lax.div(lane1, 64)
            ids = jnp.where(place < OWN, source * OWN + place, -2).astype(F32)
            blocks.append(jnp.where(targets == ids, 1.0, 0.0).astype(BF16))
        return jnp.concatenate(blocks, axis=1)

    lane16 = lax.broadcasted_iota(jnp.int32, (128, 16), 1)
    sub16 = lax.broadcasted_iota(jnp.int32, (128, 16), 0)
    param = (lane16 < 5) | ((lane16 >= 8) & (lane16 < 12))
    mine = param & (sub16 >= 64) & (sub16 < 64 + OWN)

    def read_first(at):
        return lambda other: [first_msg[c, other, MSG * at : MSG * (at + 1), :] for c in range(2)]

    precond = jnp.where(param, camera_sums(read_first(0), same), 0.0) + LAMBDA
    res0 = camera_sums(read_first(1), owned)
    dir0 = res0 / precond

    def apply(it, vec, scalars):
        cols = [jnp.broadcast_to(vec[:BLK, column_of(j) : column_of(j) + 1], (BLK, SLOTS)) for j in range(9)]
        for r in range(2):
            e = jcm[9 * r] * cols[0]
            for j in range(1, 9):
                e = e + jcm[9 * r + j] * cols[j]
            e_ref[r] = e
        for a in range(3):
            t_ref[a] = jpm[a] * e_ref[0] + jpm[3 + a] * e_ref[1]
        scatter(lambda k: [pair(t_ref, a, k) for a in range(3)], 3, q_part.at[it])
        q_copies = [
            remote(
                q_part.at[it, lax.rem(cam + d, NCAM)], q_recv.at[it, d - 1],
                qs.at[it, d - 1], qr.at[it, d - 1], cam_peer(d),
            )
            for d in (2, 1, 3)
        ]
        if it == 0:
            wait_all(v_copies)
            v = v_part[cam] + v_recv[0] + v_recv[1] + v_recv[2]
            v00, v01, v02, v11, v12, v22 = [v[LQ * i : LQ * (i + 1)] for i in range(6)]
            v00, v11, v22 = v00 + MU, v11 + MU, v22 + MU
            c00 = v11 * v22 - v12 * v12
            c01 = v02 * v12 - v01 * v22
            c02 = v01 * v12 - v02 * v11
            c11 = v00 * v22 - v02 * v02
            c12 = v01 * v02 - v00 * v12
            c22 = v00 * v11 - v01 * v01
            det = v00 * c00 + v01 * c01 + v02 * c02
            for i, value in enumerate((c00, c01, c02, c11, c12, c22)):
                cof[i] = value
            cof[6] = det
        wait_all(q_copies)
        q = q_part[it, cam] + q_recv[it, 0] + q_recv[it, 1] + q_recv[it, 2]
        q0, q1, q2 = [q[LQ * i : LQ * (i + 1)] for i in range(3)]
        det = cof[6]
        w0 = (cof[0] * q0 + cof[1] * q1 + cof[2] * q2) / det
        w1 = (cof[1] * q0 + cof[3] * q1 + cof[4] * q2) / det
        w2 = (cof[2] * q0 + cof[4] * q1 + cof[5] * q2) / det
        w_full[it, cam] = jnp.concatenate([w0, w1, w2], axis=0)
        w_copies = [
            remote(w_full.at[it, cam], w_full.at[it, cam], ws.at[it, d - 1], wr.at[it, d - 1], cam_peer(d))
            for d in (2, 1, 3)
        ]
        wait_all(w_copies)
        half = NCAM * 3 * LQ
        for part, value in enumerate(split2(w_full[it].reshape(half, HI))):
            w_split[half * part : half * (part + 1)] = value.astype(BF16)

        def body(step, carry):
            for u in range(STEPS):
                k = step * STEPS + u
                product = dot_nn(w_split[...], high[k])
                product = product[:half] + product[half:]
                for c in range(3):
                    picked = jnp.zeros((LQ, CHUNK), F32)
                    for q in range(NCAM):
                        at = (3 * q + c) * LQ
                        picked = picked + product[at : at + LQ] * low_f[k, LQ * q : LQ * (q + 1), :]
                    row = jnp.sum(picked, axis=0, keepdims=True)
                    w_obs[c, pl.ds(2 * k, 1), :] = row[:, :SLOTS]
                    w_obs[c, pl.ds(2 * k + 1, 1), :] = row[:, SLOTS:]
            return carry

        lax.fori_loop(0, CHUNKS // STEPS, body, 0)
        d = [
            e_ref[r] - (jpm[3 * r] * w_obs[0] + jpm[3 * r + 1] * w_obs[1] + jpm[3 * r + 2] * w_obs[2])
            for r in range(2)
        ]
        even, odd = spread(
            [jnp.sum(jcm[j] * d[0] + jcm[9 + j] * d[1], axis=1, keepdims=True) for j in range(9)]
        )
        if scalars is not None:
            blocks = total(even[:, :8] * vec[:BLK, :8] + odd[:, :8] * vec[:BLK, 8:])
            known = scalars + [LAMBDA * total(jnp.where(mine, vec * vec, 0.0)) + blocks]
            for i, value in enumerate(known):
                odd = jnp.where((lane64 == 4) & (sub64 == i), value, odd)
        buf = msgs.at[it]
        buf[core, chip] = message(even, odd)
        gather_end(gather_start(buf, 1 + it), buf, 1 + it)

    def read_from(it):
        return lambda other: [msgs[it, c, other] for c in range(2)]

    def saved(group):
        return equal[group]

    apply(0, dir0, None)
    image0 = jnp.where(param, camera_sums(read_from(0), saved), 0.0) + LAMBDA * dir0
    rest = res0 - image0
    dir1 = rest / precond
    dots = [total(jnp.where(mine, a * b, 0.0)) for a, b in ((res0, dir0), (dir0, rest), (rest, dir1))]
    apply(1, dir1, dots)

    sc[cam] = jnp.sum(msgs[1, 0] + msgs[1, 1], axis=0)[MSG - 1 : MSG]
    sc_copies = [
        remote(sc.at[cam], sc.at[cam], ss.at[d - 1], sr.at[d - 1], cam_peer(d)) for d in (2, 1, 3)
    ]
    image1 = jnp.where(param, camera_sums(read_from(1), saved), 0.0) + LAMBDA * dir1
    wait_all(sc_copies)
    sums = sc[0] + sc[1] + sc[2] + sc[3]
    aa, bb, cc, dd = [sums[:, 64 + i : 65 + i] for i in range(4)]
    curve = aa - bb
    alpha0 = aa / curve
    keep = -bb / curve
    rz1 = keep * keep * aa + 2.0 * keep * alpha0 * bb + alpha0 * alpha0 * cc
    scale = keep + rz1 / aa
    alpha1 = rz1 / (scale * scale * curve + 2.0 * scale * alpha0 * (bb - cc) + alpha0 * alpha0 * dd)
    dir_last = scale * dir0 + alpha0 * dir1
    img_last = scale * image0 + alpha0 * image1
    sol = alpha0 * dir0 + alpha1 * dir_last
    res = keep * res0 + alpha0 * rest - alpha1 * img_last

    def to_rows(value):
        rows = jnp.concatenate([value, jnp.zeros((128, 112), F32)], axis=1).T[:16]
        rows = jnp.concatenate([rows[column_of(j) : column_of(j) + 1] for j in range(9)], axis=0)
        return rows[:, 64 : 64 + OWN]

    sol_ref[...] = to_rows(sol)
    res_ref[...] = to_rows(res)
    for copy in pending:
        copy.wait_send()


def local(jac_cam, jac_point, point_ids, block_cam, block_fill, rhs):
    dma = pltpu.SemaphoreType.DMA
    vmem = pl.BlockSpec(memory_space=pltpu.VMEM)
    hbm = pl.BlockSpec(memory_space=pltpu.HBM)
    own = jax.ShapeDtypeStruct((9, OWN), F32)
    return pl.pallas_call(
        kernel,
        out_shape=(own, own),
        in_specs=[hbm] * 6,
        out_specs=(vmem, vmem),
        scratch_shapes=[
            pltpu.VMEM((18, BLK, SLOTS), F32),
            pltpu.VMEM((6, BLK, SLOTS), F32),
            pltpu.VMEM((BLK, SLOTS), jnp.int32),
            pltpu.VMEM((1, BLK), jnp.int32),
            pltpu.VMEM((1, BLK), jnp.int32),
            pltpu.VMEM((9, OWN), F32),
            pltpu.VMEM((CHUNKS, LO, CHUNK), BF16),
            pltpu.VMEM((CHUNKS, LO, CHUNK), F32),
            pltpu.VMEM((CHUNKS, HI, CHUNK), BF16),
            pltpu.VMEM((NCHIP // GROUP, 128, GROUP * 128), BF16),
            pltpu.VMEM((3, BLK, SLOTS), F32),
            pltpu.VMEM((3, BLK, SLOTS), F32),
            pltpu.VMEM((2, BLK, SLOTS), F32),
            pltpu.VMEM((NCAM, 6 * LQ, HI), F32),
            pltpu.VMEM((NCAM - 1, 6 * LQ, HI), F32),
            pltpu.VMEM((7, LQ, HI), F32),
            pltpu.VMEM((2, NCAM, 3 * LQ, HI), F32),
            pltpu.VMEM((2, NCAM - 1, 3 * LQ, HI), F32),
            pltpu.VMEM((2, NCAM, 3 * LQ, HI), F32),
            pltpu.VMEM((2 * NCAM * 3 * LQ, HI), BF16),
            pltpu.VMEM((2, NCHIP, 2 * MSG, 128), F32),
            pltpu.VMEM((2, 2, NCHIP, MSG, 128), F32),
            pltpu.VMEM((NCAM, 1, 128), F32),
            dma((6,)),
            dma((3, NCHIP - 1)),
            dma((3, NCHIP - 1)),
            dma((3,)),
            dma((3,)),
            dma((NCAM - 1,)),
            dma((NCAM - 1,)),
            dma((2, NCAM - 1)),
            dma((2, NCAM - 1)),
            dma((2, NCAM - 1)),
            dma((2, NCAM - 1)),
            dma((NCAM - 1,)),
            dma((NCAM - 1,)),
        ],
        compiler_params=pltpu.CompilerParams(
            collective_id=0, has_side_effects=True, vmem_limit_bytes=40 * 1024 * 1024
        ),
        name="schur_cg",
    )(jac_cam, jac_point, point_ids, block_cam.reshape(1, BLK), block_fill.reshape(1, BLK), rhs)


def solution(mesh):
    placed = (
        P(None, ("slab", "cam"), None),
        P(None, ("slab", "cam"), None),
        P(("slab", "cam"), None),
        P(("slab", "cam")),
        P(("slab", "cam")),
        P(None, ("slab", "cam")),
    )
    return jax.shard_map(
        local,
        mesh=mesh,
        in_specs=placed,
        out_specs=(P(None, ("slab", "cam")), P(None, ("slab", "cam"))),
        check_vma=False,
    )
```

time: 104 us -> 73.4 us (0.71)
  Pallas kernels: 97.7 us -> 67.2 us
    pallas_call x1, Pallas kernels: 97.7 us -> 67.2 us  [local(): pl.pallas_call(kernel, out_shape=(own, own), in_specs=[hbm] * 6, out_spec...]
where the time goes in v2:
time: 73.4 us; the launch traced here: 73.2 us
  Pallas kernels  67.2 us (92%)
  local copies, waits for them, and re-layouts  5.3 us (7%)
    pallas_call x1, Pallas kernels, local(): pl.pallas_call(kernel, out_shape=(own, own), in_specs=[hbm] * 6, out_spec...  67.2 us
    unnamed x14, local copies, waits for them, and re-layouts  5.3 us

profile of v2, /device:TPU:1, one launch (start us, length us, event | category | flops | bytes accessed | tf_op | source)
XLA Modules:
  0.0 73.2 jit_solution(10728133313506364209)
XLA Ops:
  0.6 0.0 copy-start.4
  0.6 0.0 copy-start.5
  0.7 0.6 copy-done.4
  1.3 0.0 copy-done.5
  1.3 0.0 copy-start
  1.3 1.1 %copy-done = f32[18,64,128]{2,1,0:T(8,128)S(1)} copy-done((f32[18,64,128]{2,1,0:T(8,128)S(1)}, f32[18,64,128]{2,1,0:T(8,128)}, u32[]{:S(2)}) %copy-start) | copy-done | bytes 589848
  2.4 0.0 copy-start.1
  2.4 0.9 %copy-done.1 = f32[6,64,128]{2,1,0:T(8,128)S(1)} copy-done((f32[6,64,128]{2,1,0:T(8,128)S(1)}, f32[6,64,128]{2,1,0:T(8,128)}, u32[]{:S(2)}) %copy-start.1) | copy-done | bytes 196632
  3.3 0.0 copy-start.2
  3.3 0.8 %copy-done.2 = s32[64,128]{1,0:T(8,128)S(1)} copy-done((s32[64,128]{1,0:T(8,128)S(1)}, s32[64,128]{1,0:T(8,128)}, u32[]{:S(2)}) %copy-start.2) | copy-done | bytes 32792
  4.1 0.0 copy-start.3
  4.1 0.7 copy-done.3
  4.8 67.2 %schur_cg.1 = (f32[9,48]{1,0:T(8,128)S(1)}, f32[9,48]{1,0:T(8,128)S(1)}) custom-call(f32[18,64,128]{2,1,0:T(8,128)S(1)} %copy-done, f32[6,64,128]{2,1,0:T(8,128)S(1)} %copy-done.1, s32[64,128]{1,0:T(8,128)S(1)} %copy-done.2, s32[1,64]{1,0:T(1,128)S(1)} %bitcast.2, s32[1,64]{1,0:T(1,128)S(1)} %bitcast.3, f32[9,48]{1,0:T(8,128)S(1)} %copy-done.3), custom_call_target="tpu_custom_call" | custom-call | tf_op jit(solution)/shard_map/schur_cg/pallas_call | solution.py:422
  72.0 0.6 copy.10
  72.6 0.6 copy.11
Async XLA Ops:
  0.6 0.7 copy-start.4
  0.6 0.7 copy-start.5
  1.3 1.1 %copy-start = (f32[18,64,128]{2,1,0:T(8,128)S(1)}, f32[18,64,128]{2,1,0:T(8,128)}, u32[]{:S(2)}) copy-start(f32[18,64,128]{2,1,0:T(8,128)} %jc_hbm.1) | copy-start | bytes 1769476
  2.4 0.9 %copy-start.1 = (f32[6,64,128]{2,1,0:T(8,128)S(1)}, f32[6,64,128]{2,1,0:T(8,128)}, u32[]{:S(2)}) copy-start(f32[6,64,128]{2,1,0:T(8,128)} %jp_hbm.1) | copy-start | bytes 589828
  3.3 0.8 %copy-start.2 = (s32[64,128]{1,0:T(8,128)S(1)}, s32[64,128]{1,0:T(8,128)}, u32[]{:S(2)}) copy-start(s32[64,128]{1,0:T(8,128)} %pid_hbm.1) | copy-start | bytes 98308
  4.1 0.7 copy-start.3

commit v3 on v2

--- a/solution.py
+++ b/solution.py
@@ -14,6 +14,7 @@
 
 BLK = 64
 SLOTS = 128
+ITERS = 2
 OWN = 48
 NX = 4
 NZ = 8
@@ -24,9 +25,12 @@
 LQ = LO // NCAM
 CHUNK = 256
 CHUNKS = BLK * SLOTS // CHUNK
-STEPS = 8
+STEPS_V = 4
+STEPS_Q = 16
+STEPS_W = 16
 MSG = 5
 GROUP = 4
+GROUPS = NCHIP // (2 * GROUP)
 
 NT = (((1,), (1,)), ((), ()))
 
@@ -73,8 +77,8 @@
 def kernel(
     jc_hbm, jp_hbm, pid_hbm, cam_hbm, fill_hbm, rhs_hbm, sol_ref, res_ref,
     jcm, jpm, pid_ref, cam_ref, fill_ref, rhs_ref, low_b, low_f, high, equal, t_ref, w_obs, e_ref,
-    v_part, v_recv, cof, q_part, q_recv, w_full, w_split, first_msg, msgs, sc,
-    ins, cs, cr, ps, pr, vs, vr, qs, qr, ws, wr, ss, sr,
+    v_part, v_recv, vinv, q_part, q_recv, w_full, w_split, first_msg, msgs, sc,
+    precond_ref, vecs, images, dots_ref, ins, cs, cr, ps, pr, vs, vr, qs, qr, ws, wr, ss, sr,
 ):
     slab = lax.axis_index("slab")
     cam = lax.axis_index("cam")
@@ -111,44 +115,64 @@
         pl.semaphore_signal(barrier, inc=1, device_id=cam_peer(d), device_id_type=MESH)
     pl.semaphore_signal(barrier, inc=1, device_id=sibling, device_id_type=MESH)
 
-    pending = []
-
     def remote(src, dst, send, recv, device):
         copy = pltpu.make_async_remote_copy(
             src_ref=src, dst_ref=dst, send_sem=send, recv_sem=recv, device_id=device, device_id_type=MESH
         )
         copy.start()
-        pending.append(copy)
         return copy
+
+    def received(ref, send, recv, device):
+        return pltpu.make_async_remote_copy(
+            src_ref=ref, dst_ref=ref, send_sem=send, recv_sem=recv, device_id=device, device_id_type=MESH
+        )
 
     def wait_all(copies):
         for copy in copies:
             copy.wait_recv()
 
+    def sent(copies):
+        for copy in copies:
+            copy.wait_send()
+
+    last = NCHIP - 1
+
     def gather_start(buf, m):
-        mine = buf.at[core, chip]
-        return [
-            remote(mine, mine, cs.at[m, i], cr.at[m, i], chip_peer(offset)) for i, offset in enumerate(OFFSETS)
+        for i, offset in enumerate(OFFSETS):
+            remote(buf.at[core, last], buf.at[core, i], cs.at[m], cr.at[m], chip_peer(offset))
+
+    def gather_middle(buf, m):
+        others = buf.at[core, pl.ds(0, last)]
+        received(others, cs.at[m], cr.at[m], sibling).wait_recv()
+        return remote(buf.at[core], buf.at[core], ps.at[m], pr.at[m], sibling)
+
+    def gather_sent(buf, m):
+        others = buf.at[core, pl.ds(0, last)]
+        received(others, cs.at[m], cr.at[m], sibling).wait_send()
+
+    lane8 = lax.broadcasted_iota(jnp.int32, (8, 128), 1)
+
+    def side_by_side(first, second):
+        first, second = [
+            jnp.concatenate([v, jnp.zeros((8 - MSG, 128), F32)], axis=0) for v in (first, second)
         ]
-
-    def gather_end(copies, buf, m):
-        wait_all(copies)
-        remote(buf.at[core], buf.at[core], ps.at[m], pr.at[m], sibling).wait_recv()
-
-    lane8 = lax.broadcasted_iota(jnp.int32, (8, 128), 1)
-
-    def both_cores(zero, one):
-        zero, one = [jnp.concatenate([v, jnp.zeros((8 - MSG, 128), F32)], axis=0) for v in (zero, one)]
-        even = jnp.where(lane8 < 64, zero, pltpu.roll(one, 64, 1))
-        odd = jnp.where(lane8 < 64, pltpu.roll(zero, 64, 1), one)
+        even = jnp.where(lane8 < 64, first, pltpu.roll(second, 64, 1))
+        odd = jnp.where(lane8 < 64, pltpu.roll(first, 64, 1), second)
         return jnp.concatenate([even, odd], axis=0)
 
-    def camera_sums(read, matrix):
-        acc = jnp.zeros((128, 48), F32)
-        for group in range(NCHIP // GROUP):
-            wide = jnp.concatenate([both_cores(*read(GROUP * group + p)) for p in range(GROUP)], axis=1)
+    def camera_sums(read, matrix, acc, of_core):
+        for group in range(GROUPS):
+            slots = range(2 * GROUP * group, 2 * GROUP * (group + 1), 2)
+            wide = jnp.concatenate(
+                [side_by_side(read(of_core, slot), read(of_core, slot + 1)) for slot in slots], axis=1
+            )
             parts = jnp.concatenate(split3(wide), axis=0).astype(BF16)
-            acc = acc + dot_nt(matrix(group), parts)
+            acc = acc + dot_nt(matrix(of_core, group), parts)
+        return acc
+
+    zero_sums = jnp.zeros((128, 48), F32)
+
+    def three_parts(acc):
         return acc[:, 0:16] + acc[:, 16:32] + acc[:, 32:48]
 
     def column(row):
@@ -193,7 +217,7 @@
     none = jnp.zeros((1, OWN), F32)
     rhs_even = jnp.concatenate([rhs[j : j + 1] for j in range(0, 9, 2)], axis=0)
     rhs_odd = jnp.concatenate([rhs[j : j + 1] for j in range(1, 9, 2)] + [none], axis=0)
-    first_msg[core, chip] = jnp.concatenate(
+    first_msg[core, last] = jnp.concatenate(
         [message(even, odd), jnp.concatenate([rhs_even, gap, rhs_odd, gap], axis=1)], axis=0
     )
 
@@ -216,19 +240,19 @@
         jpm[i] = jnp.where(live, jpm[i], 0.0)
 
     pl.semaphore_wait(barrier, len(OFFSETS) + NCAM)
-    first_copies = gather_start(first_msg, 0)
+    gather_start(first_msg, 0)
 
     def pair(ref, index, k):
         return jnp.concatenate([ref[index, pl.ds(2 * k, 1), :], ref[index, pl.ds(2 * k + 1, 1), :]], axis=1)
 
-    def scatter(rows_of, count, acc_ref):
+    def scatter(rows_of, count, acc_ref, steps):
         half = NCAM * count * LQ
         acc_ref[...] = jnp.zeros_like(acc_ref)
 
         def body(step, carry):
             summed = None
-            for u in range(STEPS):
-                k = step * STEPS + u
+            for u in range(steps):
+                k = step * steps + u
                 parts = [], []
                 for row in rows_of(k):
                     for part, value in zip(parts, split2(row)):
@@ -244,39 +268,48 @@
             acc_ref[...] += (summed[:half] + summed[half:]).reshape(NCAM, count * LQ, HI)
             return carry
 
-        lax.fori_loop(0, CHUNKS // STEPS, body, 0)
+        lax.fori_loop(0, CHUNKS // steps, body, 0)
 
     def jp_products(k):
         a = [pair(jpm, i, k) for i in range(6)]
         return [a[i] * a[j] + a[3 + i] * a[3 + j] for i, j in ((0, 0), (0, 1), (0, 2), (1, 1), (1, 2), (2, 2))]
 
-    scatter(jp_products, 6, v_part)
+    scatter(jp_products, 6, v_part, STEPS_V)
+    first_swap = gather_middle(first_msg, 0)
     v_copies = [
         remote(v_part.at[lax.rem(cam + d, NCAM)], v_recv.at[d - 1], vs.at[d - 1], vr.at[d - 1], cam_peer(d))
         for d in range(1, NCAM)
     ]
 
-    gather_end(first_copies, first_msg, 0)
     lane1 = lax.broadcasted_iota(jnp.int32, (1, 128), 1)
 
-    def same(group):
+    def same(of_core, group):
         blocks = []
         for p in range(GROUP):
-            zero, one = [first_msg[c, GROUP * group + p, MSG - 1 : MSG, :] for c in range(2)]
-            ids = jnp.where(lane1 < 64, pltpu.roll(zero, 64, 1), one)
+            slot = 2 * (GROUP * group + p)
+            first, second = [first_msg[of_core, slot + i, MSG - 1 : MSG, :] for i in range(2)]
+            ids = jnp.where(lane1 < 64, pltpu.roll(first, 64, 1), second)
             blocks.append(jnp.where(targets == ids, 1.0, 0.0).astype(BF16))
         matrix = jnp.concatenate(blocks, axis=1)
-        equal[group] = matrix
+        equal[of_core, group] = matrix
         return matrix
 
-    def owned(group):
+    def owned(of_core, group):
         place = lax.rem(lane1, 64)
         blocks = []
         for p in range(GROUP):
-            source = (GROUP * group + p) * 2 + lax.div(lane1, 64)
+            slot = 2 * (GROUP * group + p)
+            first, second = [
+                lax.rem(x - dx + NX, NX) * NZ + lax.rem(z - dz + NZ, NZ)
+                for dx, dz in (OFFSETS + [(0, 0)])[slot : slot + 2]
+            ]
+            source = jnp.where(lane1 < 64, first, second) * 2 + of_core
             ids = jnp.where(place < OWN, source * OWN + place, -2).astype(F32)
             blocks.append(jnp.where(targets == ids, 1.0, 0.0).astype(BF16))
         return jnp.concatenate(blocks, axis=1)
+
+    def saved(of_core, group):
+        return equal[of_core, group]
 
     lane16 = lax.broadcasted_iota(jnp.int32, (128, 16), 1)
     sub16 = lax.broadcasted_iota(jnp.int32, (128, 16), 0)
@@ -284,13 +317,22 @@
     mine = param & (sub16 >= 64) & (sub16 < 64 + OWN)
 
     def read_first(at):
-        return lambda other: [first_msg[c, other, MSG * at : MSG * (at + 1), :] for c in range(2)]
-
-    precond = jnp.where(param, camera_sums(read_first(0), same), 0.0) + LAMBDA
-    res0 = camera_sums(read_first(1), owned)
-    dir0 = res0 / precond
-
-    def apply(it, vec, scalars):
+        return lambda of_core, slot: first_msg[of_core, slot, MSG * at : MSG * (at + 1), :]
+
+    diag_sums = camera_sums(read_first(0), same, zero_sums, core)
+    rhs_sums = camera_sums(read_first(1), owned, zero_sums, core)
+    first_swap.wait_recv()
+    diag_sums = camera_sums(read_first(0), same, diag_sums, 1 - core)
+    rhs_sums = camera_sums(read_first(1), owned, rhs_sums, 1 - core)
+    precond = jnp.where(param, three_parts(diag_sums), 0.0) + LAMBDA
+    res0 = three_parts(rhs_sums)
+    precond_ref[...] = precond
+    vecs[0] = res0 / precond
+    vecs[1] = res0
+    dots_ref[...] = jnp.zeros((1, 128), F32)
+
+    def apply(it, carry):
+        vec = vecs[it]
         cols = [jnp.broadcast_to(vec[:BLK, column_of(j) : column_of(j) + 1], (BLK, SLOTS)) for j in range(9)]
         for r in range(2):
             e = jcm[9 * r] * cols[0]
@@ -299,7 +341,7 @@
             e_ref[r] = e
         for a in range(3):
             t_ref[a] = jpm[a] * e_ref[0] + jpm[3 + a] * e_ref[1]
-        scatter(lambda k: [pair(t_ref, a, k) for a in range(3)], 3, q_part.at[it])
+        scatter(lambda k: [pair(t_ref, a, k) for a in range(3)], 3, q_part.at[it], STEPS_Q)
         q_copies = [
             remote(
                 q_part.at[it, lax.rem(cam + d, NCAM)], q_recv.at[it, d - 1],
@@ -307,7 +349,11 @@
             )
             for d in (2, 1, 3)
         ]
-        if it == 0:
+        square = LAMBDA * total(jnp.where(mine, vec * vec, 0.0))
+        square = square + total(e_ref[0] * e_ref[0] + e_ref[1] * e_ref[1])
+
+        @pl.when(it == 0)
+        def invert():
             wait_all(v_copies)
             v = v_part[cam] + v_recv[0] + v_recv[1] + v_recv[2]
             v00, v01, v02, v11, v12, v22 = [v[LQ * i : LQ * (i + 1)] for i in range(6)]
@@ -320,18 +366,23 @@
             c22 = v00 * v11 - v01 * v01
             det = v00 * c00 + v01 * c01 + v02 * c02
             for i, value in enumerate((c00, c01, c02, c11, c12, c22)):
-                cof[i] = value
-            cof[6] = det
+                vinv[i] = value / det
+
         wait_all(q_copies)
         q = q_part[it, cam] + q_recv[it, 0] + q_recv[it, 1] + q_recv[it, 2]
         q0, q1, q2 = [q[LQ * i : LQ * (i + 1)] for i in range(3)]
-        det = cof[6]
-        w0 = (cof[0] * q0 + cof[1] * q1 + cof[2] * q2) / det
-        w1 = (cof[1] * q0 + cof[3] * q1 + cof[4] * q2) / det
-        w2 = (cof[2] * q0 + cof[4] * q1 + cof[5] * q2) / det
+        w0 = vinv[0] * q0 + vinv[1] * q1 + vinv[2] * q2
+        w1 = vinv[1] * q0 + vinv[3] * q1 + vinv[4] * q2
+        w2 = vinv[2] * q0 + vinv[4] * q1 + vinv[5] * q2
         w_full[it, cam] = jnp.concatenate([w0, w1, w2], axis=0)
         w_copies = [
             remote(w_full.at[it, cam], w_full.at[it, cam], ws.at[it, d - 1], wr.at[it, d - 1], cam_peer(d))
+            for d in (2, 1, 3)
+        ]
+        square = square - total(q0 * w0 + q1 * w1 + q2 * w2)
+        sc[it, cam] = jnp.where(lane1 == 3, square, dots_ref[...])
+        sc_copies = [
+            remote(sc.at[it, cam], sc.at[it, cam], ss.at[it, d - 1], sr.at[it, d - 1], cam_peer(d))
             for d in (2, 1, 3)
         ]
         wait_all(w_copies)
@@ -340,8 +391,8 @@
             w_split[half * part : half * (part + 1)] = value.astype(BF16)
 
         def body(step, carry):
-            for u in range(STEPS):
-                k = step * STEPS + u
+            for u in range(STEPS_W):
+                k = step * STEPS_W + u
                 product = dot_nn(w_split[...], high[k])
                 product = product[:half] + product[half:]
                 for c in range(3):
@@ -354,7 +405,7 @@
                     w_obs[c, pl.ds(2 * k + 1, 1), :] = row[:, SLOTS:]
             return carry
 
-        lax.fori_loop(0, CHUNKS // STEPS, body, 0)
+        lax.fori_loop(0, CHUNKS // STEPS_W, body, 0)
         d = [
             e_ref[r] - (jpm[3 * r] * w_obs[0] + jpm[3 * r + 1] * w_obs[1] + jpm[3 * r + 2] * w_obs[2])
             for r in range(2)
@@ -362,35 +413,45 @@
         even, odd = spread(
             [jnp.sum(jcm[j] * d[0] + jcm[9 + j] * d[1], axis=1, keepdims=True) for j in range(9)]
         )
-        if scalars is not None:
-            blocks = total(even[:, :8] * vec[:BLK, :8] + odd[:, :8] * vec[:BLK, 8:])
-            known = scalars + [LAMBDA * total(jnp.where(mine, vec * vec, 0.0)) + blocks]
-            for i, value in enumerate(known):
-                odd = jnp.where((lane64 == 4) & (sub64 == i), value, odd)
+        wait_all(sc_copies)
+        sums = column((sc[it, 0] + sc[it, 1] + sc[it, 2] + sc[it, 3])[:, :64])[:BLK]
+        odd = jnp.where((lane64 == 4) & (sub64 < 4), sums, odd)
         buf = msgs.at[it]
-        buf[core, chip] = message(even, odd)
-        gather_end(gather_start(buf, 1 + it), buf, 1 + it)
-
-    def read_from(it):
-        return lambda other: [msgs[it, c, other] for c in range(2)]
-
-    def saved(group):
-        return equal[group]
-
-    apply(0, dir0, None)
-    image0 = jnp.where(param, camera_sums(read_from(0), saved), 0.0) + LAMBDA * dir0
+        buf[core, last] = message(even, odd)
+        gather_start(buf, 1 + it)
+        sent(q_copies + w_copies + sc_copies)
+        swap = gather_middle(buf, 1 + it)
+
+        def read(of_core, slot):
+            return msgs[it, of_core, slot]
+
+        acc = camera_sums(read, saved, zero_sums, core)
+        swap.wait_recv()
+        acc = camera_sums(read, saved, acc, 1 - core)
+        image = jnp.where(param, three_parts(acc), 0.0) + LAMBDA * vec
+        images[it] = image
+
+        @pl.when(it == 0)
+        def prepare():
+            res0 = vecs[1]
+            rest = res0 - image
+            following = rest / precond_ref[...]
+            row = jnp.zeros((1, 128), F32)
+            for i, (a, b) in enumerate(((res0, vec), (vec, rest), (rest, following))):
+                row = jnp.where(lane1 == i, total(jnp.where(mine, a * b, 0.0)), row)
+            dots_ref[...] = row
+            vecs[1] = following
+            vecs[2] = res0
+
+        swap.wait_send()
+        gather_sent(buf, 1 + it)
+        return carry
+
+    lax.fori_loop(0, ITERS, apply, 0)
+    dir0, dir1, res0 = vecs[0], vecs[1], vecs[2]
+    image0, image1 = images[0], images[1]
     rest = res0 - image0
-    dir1 = rest / precond
-    dots = [total(jnp.where(mine, a * b, 0.0)) for a, b in ((res0, dir0), (dir0, rest), (rest, dir1))]
-    apply(1, dir1, dots)
-
-    sc[cam] = jnp.sum(msgs[1, 0] + msgs[1, 1], axis=0)[MSG - 1 : MSG]
-    sc_copies = [
-        remote(sc.at[cam], sc.at[cam], ss.at[d - 1], sr.at[d - 1], cam_peer(d)) for d in (2, 1, 3)
-    ]
-    image1 = jnp.where(param, camera_sums(read_from(1), saved), 0.0) + LAMBDA * dir1
-    wait_all(sc_copies)
-    sums = sc[0] + sc[1] + sc[2] + sc[3]
+    sums = jnp.sum(msgs[1, 0] + msgs[1, 1], axis=0)[MSG - 1 : MSG]
     aa, bb, cc, dd = [sums[:, 64 + i : 65 + i] for i in range(4)]
     curve = aa - bb
     alpha0 = aa / curve
@@ -410,8 +471,8 @@
 
     sol_ref[...] = to_rows(sol)
     res_ref[...] = to_rows(res)
-    for copy in pending:
-        copy.wait_send()
+    sent(v_copies + [first_swap])
+    gather_sent(first_msg, 0)
 
 
 def local(jac_cam, jac_point, point_ids, block_cam, block_fill, rhs):
@@ -434,23 +495,27 @@
             pltpu.VMEM((CHUNKS, LO, CHUNK), BF16),
             pltpu.VMEM((CHUNKS, LO, CHUNK), F32),
             pltpu.VMEM((CHUNKS, HI, CHUNK), BF16),
-            pltpu.VMEM((NCHIP // GROUP, 128, GROUP * 128), BF16),
+            pltpu.VMEM((2, GROUPS, 128, GROUP * 128), BF16),
             pltpu.VMEM((3, BLK, SLOTS), F32),
             pltpu.VMEM((3, BLK, SLOTS), F32),
             pltpu.VMEM((2, BLK, SLOTS), F32),
             pltpu.VMEM((NCAM, 6 * LQ, HI), F32),
             pltpu.VMEM((NCAM - 1, 6 * LQ, HI), F32),
-            pltpu.VMEM((7, LQ, HI), F32),
+            pltpu.VMEM((6, LQ, HI), F32),
             pltpu.VMEM((2, NCAM, 3 * LQ, HI), F32),
             pltpu.VMEM((2, NCAM - 1, 3 * LQ, HI), F32),
             pltpu.VMEM((2, NCAM, 3 * LQ, HI), F32),
             pltpu.VMEM((2 * NCAM * 3 * LQ, HI), BF16),
             pltpu.VMEM((2, NCHIP, 2 * MSG, 128), F32),
             pltpu.VMEM((2, 2, NCHIP, MSG, 128), F32),
-            pltpu.VMEM((NCAM, 1, 128), F32),
+            pltpu.VMEM((2, NCAM, 1, 128), F32),
+            pltpu.VMEM((128, 16), F32),
+            pltpu.VMEM((3, 128, 16), F32),
+            pltpu.VMEM((2, 128, 16), F32),
+            pltpu.VMEM((1, 128), F32),
             dma((6,)),
-            dma((3, NCHIP - 1)),
-            dma((3, NCHIP - 1)),
+            dma((3,)),
+            dma((3,)),
             dma((3,)),
             dma((3,)),
             dma((NCAM - 1,)),
@@ -459,11 +524,11 @@
             dma((2, NCAM - 1)),
             dma((2, NCAM - 1)),
             dma((2, NCAM - 1)),
-            dma((NCAM - 1,)),
-            dma((NCAM - 1,)),
+            dma((2, NCAM - 1)),
+            dma((2, NCAM - 1)),
         ],
         compiler_params=pltpu.CompilerParams(
-            collective_id=0, has_side_effects=True, vmem_limit_bytes=40 * 1024 * 1024
+            collective_id=0, has_side_effects=True, vmem_limit_bytes=60 * 1024 * 1024
         ),
         name="schur_cg",
     )(jac_cam, jac_point, point_ids, block_cam.reshape(1, BLK), block_fill.reshape(1, BLK), rhs)

time: 73.4 us -> 65.6 us (0.89)
  Pallas kernels: 67.2 us -> 62.9 us
  local copies, waits for them, and re-layouts: 5.3 us -> 1.9 us
    pallas_call x1, Pallas kernels: 67.2 us -> 62.9 us  [local(): pl.pallas_call(kernel, out_shape=(own, own), in_specs=[hbm] * 6, out_spec...]
    unnamed x14 -> x4, local copies, waits for them, and re-layouts: 5.3 us -> 1.9 us
where the time goes in v3:
time: 65.6 us; the launch traced here: 65.5 us
  Pallas kernels  62.9 us (96%)
  local copies, waits for them, and re-layouts  1.9 us (3%)
    pallas_call x1, Pallas kernels, local(): pl.pallas_call(kernel, out_shape=(own, own), in_specs=[hbm] * 6, out_spec...  62.9 us
    unnamed x4, local copies, waits for them, and re-layouts  1.9 us

profile of v3, /device:TPU:1, one launch (start us, length us, event | category | flops | bytes accessed | tf_op | source)
XLA Modules:
  0.0 65.5 jit_solution(2893979471990178486)
XLA Ops:
  0.6 62.9 %schur_cg.1 = (f32[9,48]{1,0:T(8,128)}, f32[9,48]{1,0:T(8,128)}) custom-call(f32[18,64,128]{2,1,0:T(8,128)} %jc_hbm.1, f32[6,64,128]{2,1,0:T(8,128)} %jp_hbm.1, s32[64,128]{1,0:T(8,128)} %pid_hbm.1, s32[1,64]{1,0:T(1,128)} %bitcast.2, s32[1,64]{1,0:T(1,128)} %bitcast.3, f32[9,48]{1,0:T(8,128)} %rhs_hbm.1), custom_call_target="tpu_custom_call" | custom-call | tf_op jit(solution)/shard_map/schur_cg/pallas_call | solution.py:483
  63.6 0.0 copy-start
  63.6 1.3 %copy.10 = f32[9,48]{1,0:T(8,128)} copy(f32[9,48]{1,0:T(8,128)} %get-tuple-element.4) | data formatting | bytes 3456
  64.9 0.0 copy-done
  64.9 0.6 copy.11
Async XLA Ops:
  63.6 1.3 %copy-start = (f32[9,48]{1,0:T(8,128)S(1)}, f32[9,48]{1,0:T(8,128)}, u32[]{:S(2)}) copy-start(f32[9,48]{1,0:T(8,128)} %get-tuple-element.5) | copy-start | bytes 5188

commit v4 on v3

--- a/solution.py
+++ b/solution.py
@@ -26,7 +26,7 @@
 CHUNK = 256
 CHUNKS = BLK * SLOTS // CHUNK
 STEPS_V = 4
-STEPS_Q = 16
+STEPS_Q = 32
 STEPS_W = 16
 MSG = 5
 GROUP = 4
@@ -97,6 +97,13 @@
     def cam_peer(d):
         return (slab, lax.rem(cam + d, NCAM))
 
+    barrier = pltpu.get_barrier_semaphore()
+    for offset in OFFSETS:
+        pl.semaphore_signal(barrier, inc=1, device_id=chip_peer(offset), device_id_type=MESH)
+    for d in range(1, NCAM):
+        pl.semaphore_signal(barrier, inc=1, device_id=cam_peer(d), device_id_type=MESH)
+    pl.semaphore_signal(barrier, inc=1, device_id=sibling, device_id_type=MESH)
+
     inputs = [
         pltpu.make_async_copy(src, dst, ins.at[i])
         for i, (src, dst) in enumerate(
@@ -108,13 +115,6 @@
     ]
     for copy in inputs:
         copy.start()
-    barrier = pltpu.get_barrier_semaphore()
-    for offset in OFFSETS:
-        pl.semaphore_signal(barrier, inc=1, device_id=chip_peer(offset), device_id_type=MESH)
-    for d in range(1, NCAM):
-        pl.semaphore_signal(barrier, inc=1, device_id=cam_peer(d), device_id_type=MESH)
-    pl.semaphore_signal(barrier, inc=1, device_id=sibling, device_id_type=MESH)
-
     def remote(src, dst, send, recv, device):
         copy = pltpu.make_async_remote_copy(
             src_ref=src, dst_ref=dst, send_sem=send, recv_sem=recv, device_id=device, device_id_type=MESH
@@ -475,12 +475,23 @@
     gather_sent(first_msg, 0)
 
 
+def deliver(sol_in, res_in, sol_out, res_out, sems):
+    copies = [
+        pltpu.make_async_copy(src, dst, sems.at[i])
+        for i, (src, dst) in enumerate(((sol_in, sol_out), (res_in, res_out)))
+    ]
+    for copy in copies:
+        copy.start()
+    for copy in copies:
+        copy.wait()
+
+
 def local(jac_cam, jac_point, point_ids, block_cam, block_fill, rhs):
     dma = pltpu.SemaphoreType.DMA
     vmem = pl.BlockSpec(memory_space=pltpu.VMEM)
     hbm = pl.BlockSpec(memory_space=pltpu.HBM)
     own = jax.ShapeDtypeStruct((9, OWN), F32)
-    return pl.pallas_call(
+    outputs = pl.pallas_call(
         kernel,
         out_shape=(own, own),
         in_specs=[hbm] * 6,
@@ -532,6 +543,14 @@
         ),
         name="schur_cg",
     )(jac_cam, jac_point, point_ids, block_cam.reshape(1, BLK), block_fill.reshape(1, BLK), rhs)
+    return pl.pallas_call(
+        deliver,
+        out_shape=(own, own),
+        in_specs=[vmem] * 2,
+        out_specs=(hbm, hbm),
+        scratch_shapes=[dma((2,))],
+        name="deliver",
+    )(*outputs)
 
 
 def solution(mesh):

time: 65.6 us -> 64.4 us (0.982)
  local copies, waits for them, and re-layouts: 1.9 us -> 0 us
  Pallas kernels: 62.9 us -> 63.6 us
    unnamed x4 -> x0, local copies, waits for them, and re-layouts: 1.9 us -> none
    pallas_call x0 -> x1, Pallas kernels: none -> 1.33 us  [local(): pl.pallas_call(deliver, out_shape=(own, own), in_specs=[vmem] * 2, out_sp...]
    pallas_call x1, Pallas kernels: 62.9 us -> 62.3 us  [local(): pl.pallas_call(kernel, out_shape=(own, own), in_specs=[hbm] * 6, out_spec...]
where the time goes in v4:
time: 64.4 us; the launch traced here: 64.2 us
  Pallas kernels  63.6 us (99%)
    pallas_call x1, Pallas kernels, local(): pl.pallas_call(kernel, out_shape=(own, own), in_specs=[hbm] * 6, out_spec...  62.3 us
    pallas_call x1, Pallas kernels, local(): pl.pallas_call(deliver, out_shape=(own, own), in_specs=[vmem] * 2, out_sp...  1.33 us

profile of v4, /device:TPU:1, one launch (start us, length us, event | category | flops | bytes accessed | tf_op | source)
XLA Modules:
  0.0 64.2 jit_solution(6377416313506333769)
XLA Ops:
  0.6 62.3 %schur_cg.1 = (f32[9,48]{1,0:T(8,128)}, f32[9,48]{1,0:T(8,128)}) custom-call(f32[18,64,128]{2,1,0:T(8,128)} %jc_hbm.1, f32[6,64,128]{2,1,0:T(8,128)} %jp_hbm.1, s32[64,128]{1,0:T(8,128)} %pid_hbm.1, s32[1,64]{1,0:T(1,128)} %bitcast.2, s32[1,64]{1,0:T(1,128)} %bitcast.3, f32[9,48]{1,0:T(8,128)} %rhs_hbm.1), custom_call_target="tpu_custom_call" | custom-call | tf_op jit(solution)/shard_map/schur_cg/pallas_call | solution.py:494
  62.9 1.3 %deliver.1 = (f32[9,48]{1,0:T(8,128)}, f32[9,48]{1,0:T(8,128)}) custom-call(f32[9,48]{1,0:T(8,128)} %get-tuple-element.4.sol_in, f32[9,48]{1,0:T(8,128)} %get-tuple-element.5.res_in), custom_call_target="tpu_custom_call" | custom-call | tf_op jit(solution)/shard_map/deliver/pallas_call | solution.py:546

commit v5 on v4

--- a/solution.py
+++ b/solution.py
@@ -25,7 +25,7 @@
 LQ = LO // NCAM
 CHUNK = 256
 CHUNKS = BLK * SLOTS // CHUNK
-STEPS_V = 4
+STEPS_V = 8
 STEPS_Q = 32
 STEPS_W = 16
 MSG = 5
@@ -76,7 +76,7 @@
 
 def kernel(
     jc_hbm, jp_hbm, pid_hbm, cam_hbm, fill_hbm, rhs_hbm, sol_ref, res_ref,
-    jcm, jpm, pid_ref, cam_ref, fill_ref, rhs_ref, low_b, low_f, high, equal, t_ref, w_obs, e_ref,
+    jcm, jpm, pid_ref, cam_ref, fill_ref, rhs_ref, low_b, low_f, high, equal, holds, t_ref, w_obs, e_ref,
     v_part, v_recv, vinv, q_part, q_recv, w_full, w_split, first_msg, msgs, sc,
     precond_ref, vecs, images, dots_ref, ins, cs, cr, ps, pr, vs, vr, qs, qr, ws, wr, ss, sr,
 ):
@@ -241,6 +241,25 @@
 
     pl.semaphore_wait(barrier, len(OFFSETS) + NCAM)
     gather_start(first_msg, 0)
+    lane1 = lax.broadcasted_iota(jnp.int32, (1, 128), 1)
+
+    def owner_matrix(of_core, group):
+        place = lax.rem(lane1, 64)
+        blocks = []
+        for p in range(GROUP):
+            slot = 2 * (GROUP * group + p)
+            first, second = [
+                lax.rem(x - dx + NX, NX) * NZ + lax.rem(z - dz + NZ, NZ)
+                for dx, dz in (OFFSETS + [(0, 0)])[slot : slot + 2]
+            ]
+            source = jnp.where(lane1 < 64, first, second) * 2 + of_core
+            ids = jnp.where(place < OWN, source * OWN + place, -2).astype(F32)
+            blocks.append(jnp.where(targets == ids, 1.0, 0.0).astype(BF16))
+        return jnp.concatenate(blocks, axis=1)
+
+    for of_core in range(2):
+        for group in range(GROUPS):
+            holds[of_core, group] = owner_matrix(of_core, group)
 
     def pair(ref, index, k):
         return jnp.concatenate([ref[index, pl.ds(2 * k, 1), :], ref[index, pl.ds(2 * k + 1, 1), :]], axis=1)
@@ -281,7 +300,6 @@
         for d in range(1, NCAM)
     ]
 
-    lane1 = lax.broadcasted_iota(jnp.int32, (1, 128), 1)
 
     def same(of_core, group):
         blocks = []
@@ -295,18 +313,7 @@
         return matrix
 
     def owned(of_core, group):
-        place = lax.rem(lane1, 64)
-        blocks = []
-        for p in range(GROUP):
-            slot = 2 * (GROUP * group + p)
-            first, second = [
-                lax.rem(x - dx + NX, NX) * NZ + lax.rem(z - dz + NZ, NZ)
-                for dx, dz in (OFFSETS + [(0, 0)])[slot : slot + 2]
-            ]
-            source = jnp.where(lane1 < 64, first, second) * 2 + of_core
-            ids = jnp.where(place < OWN, source * OWN + place, -2).astype(F32)
-            blocks.append(jnp.where(targets == ids, 1.0, 0.0).astype(BF16))
-        return jnp.concatenate(blocks, axis=1)
+        return holds[of_core, group]
 
     def saved(of_core, group):
         return equal[of_core, group]
@@ -385,15 +392,21 @@
             remote(sc.at[it, cam], sc.at[it, cam], ss.at[it, d - 1], sr.at[it, d - 1], cam_peer(d))
             for d in (2, 1, 3)
         ]
-        wait_all(w_copies)
         half = NCAM * 3 * LQ
-        for part, value in enumerate(split2(w_full[it].reshape(half, HI))):
-            w_split[half * part : half * (part + 1)] = value.astype(BF16)
+
+        def keep_split(peer):
+            for part, value in enumerate(split2(w_full[it, peer])):
+                w_split[part, peer] = value.astype(BF16)
+
+        keep_split(cam)
+        for copy, d in ((w_copies[1], 1), (w_copies[2], 3), (w_copies[0], 2)):
+            copy.wait_recv()
+            keep_split(lax.rem(cam + NCAM - d, NCAM))
 
         def body(step, carry):
             for u in range(STEPS_W):
                 k = step * STEPS_W + u
-                product = dot_nn(w_split[...], high[k])
+                product = dot_nn(w_split[...].reshape(2 * half, HI), high[k])
                 product = product[:half] + product[half:]
                 for c in range(3):
                     picked = jnp.zeros((LQ, CHUNK), F32)
@@ -414,10 +427,11 @@
             [jnp.sum(jcm[j] * d[0] + jcm[9 + j] * d[1], axis=1, keepdims=True) for j in range(9)]
         )
         wait_all(sc_copies)
-        sums = column((sc[it, 0] + sc[it, 1] + sc[it, 2] + sc[it, 3])[:, :64])[:BLK]
-        odd = jnp.where((lane64 == 4) & (sub64 < 4), sums, odd)
+        sums = pltpu.roll(sc[it, 0] + sc[it, 1] + sc[it, 2] + sc[it, 3], 64, 1)
         buf = msgs.at[it]
-        buf[core, last] = message(even, odd)
+        terms = message(even, odd)
+        extra = jnp.where((lane1 >= 64) & (lane1 < 68), sums, terms[MSG - 1 :])
+        buf[core, last] = jnp.concatenate([terms[: MSG - 1], extra], axis=0)
         gather_start(buf, 1 + it)
         sent(q_copies + w_copies + sc_copies)
         swap = gather_middle(buf, 1 + it)
@@ -464,13 +478,10 @@
     sol = alpha0 * dir0 + alpha1 * dir_last
     res = keep * res0 + alpha0 * rest - alpha1 * img_last
 
-    def to_rows(value):
-        rows = jnp.concatenate([value, jnp.zeros((128, 112), F32)], axis=1).T[:16]
-        rows = jnp.concatenate([rows[column_of(j) : column_of(j) + 1] for j in range(9)], axis=0)
-        return rows[:, 64 : 64 + OWN]
-
-    sol_ref[...] = to_rows(sol)
-    res_ref[...] = to_rows(res)
+    both = jnp.concatenate([sol, res, jnp.zeros((128, 96), F32)], axis=1).T
+    for at, out in ((0, sol_ref), (16, res_ref)):
+        rows = jnp.concatenate([both[at + column_of(j) : at + column_of(j) + 1] for j in range(9)], axis=0)
+        out[...] = rows[:, 64 : 64 + OWN]
     sent(v_copies + [first_swap])
     gather_sent(first_msg, 0)
 
@@ -507,6 +518,7 @@
             pltpu.VMEM((CHUNKS, LO, CHUNK), F32),
             pltpu.VMEM((CHUNKS, HI, CHUNK), BF16),
             pltpu.VMEM((2, GROUPS, 128, GROUP * 128), BF16),
+            pltpu.VMEM((2, GROUPS, 128, GROUP * 128), BF16),
             pltpu.VMEM((3, BLK, SLOTS), F32),
             pltpu.VMEM((3, BLK, SLOTS), F32),
             pltpu.VMEM((2, BLK, SLOTS), F32),
@@ -516,7 +528,7 @@
             pltpu.VMEM((2, NCAM, 3 * LQ, HI), F32),
             pltpu.VMEM((2, NCAM - 1, 3 * LQ, HI), F32),
             pltpu.VMEM((2, NCAM, 3 * LQ, HI), F32),
-            pltpu.VMEM((2 * NCAM * 3 * LQ, HI), BF16),
+            pltpu.VMEM((2, NCAM, 3 * LQ, HI), BF16),
             pltpu.VMEM((2, NCHIP, 2 * MSG, 128), F32),
             pltpu.VMEM((2, 2, NCHIP, MSG, 128), F32),
             pltpu.VMEM((2, NCAM, 1, 128), F32),

time: 64.4 us -> 64.4 us (level)
  no operation moved by 1% of the time
where the time goes in v5:
time: 64.4 us; the launch traced here: 64.2 us
  Pallas kernels  63.6 us (99%)
    pallas_call x1, Pallas kernels, local(): pl.pallas_call(kernel, out_shape=(own, own), in_specs=[hbm] * 6, out_spec...  62.3 us
    pallas_call x1, Pallas kernels, local(): pl.pallas_call(deliver, out_shape=(own, own), in_specs=[vmem] * 2, out_sp...  1.33 us

profile of v5, /device:TPU:1, one launch (start us, length us, event | category | flops | bytes accessed | tf_op | source)
XLA Modules:
  0.0 64.2 jit_solution(12184669162177413638)
XLA Ops:
  0.6 62.3 %schur_cg.1 = (f32[9,48]{1,0:T(8,128)}, f32[9,48]{1,0:T(8,128)}) custom-call(f32[18,64,128]{2,1,0:T(8,128)} %jc_hbm.1, f32[6,64,128]{2,1,0:T(8,128)} %jp_hbm.1, s32[64,128]{1,0:T(8,128)} %pid_hbm.1, s32[1,64]{1,0:T(1,128)} %bitcast.2, s32[1,64]{1,0:T(1,128)} %bitcast.3, f32[9,48]{1,0:T(8,128)} %rhs_hbm.1), custom_call_target="tpu_custom_call" | custom-call | tf_op jit(solution)/shard_map/schur_cg/pallas_call | solution.py:505
  62.9 1.3 %deliver.1 = (f32[9,48]{1,0:T(8,128)}, f32[9,48]{1,0:T(8,128)}) custom-call(f32[9,48]{1,0:T(8,128)} %get-tuple-element.4.sol_in, f32[9,48]{1,0:T(8,128)} %get-tuple-element.5.res_in), custom_call_target="tpu_custom_call" | custom-call | tf_op jit(solution)/shard_map/deliver/pallas_call | solution.py:558
